TPU v7x, 256 devices: a whole 4x4x8 slice. The times are simulated.
256 devices in a mesh: group: 8 (over y_hi, x), member: 32 (over z, y_lo, core).
Axes of the slice: x: 4, y: 4 (y_hi: 2, y_lo: 2; y = y_hi * 2 + y_lo), z: 8, core: 2. Of those that a mesh axis runs over, the one named last changes fastest.
Arguments:
- query_states: bfloat16 [2048, 32, 4096], P(('group', 'member')), may hold values from -6 to 6
- passage_states: bfloat16 [1024, 128, 4096], P(('group', 'member')), may hold values from -6 to 6
- projection: bfloat16 [4096, 128], replicated, may hold values from -0.09375 to 0.09375
- query_len: int32 [2048], P(('group', 'member')), may hold values from 16 to 32
- passage_len: int32 [1024], P(('group', 'member')), may hold values from 32 to 128
- neg_ids: int32 [2048, 16], P(('group', 'member')), may hold values from 0 to 1023, as said below
- neg_count: int32 [2048], P(('group', 'member')), may hold values from 1 to 16
- teacher: float32 [2048, 144], P(('group', 'member')), may hold values from -4 to 4
Outputs:
- grad_projection: float32 [4096, 128], replicated
- loss: float32 [], replicated
Inputs may be any that keep to these rules, and one draw needn't show every extreme that they name: neg_ids[q, k] names a passage of the same member index as query q in a data group other than q's.
All inputs are finite; a program needn't handle non-finite values.
Results may differ from a plain program's by a relative error of at most 0.0077.
Values may be sent and summed in bfloat16 or wider, within the bound.
No kernel may reach another device: no remote copies, remote signals or barrier semaphores. Data moves between devices by JAX's collectives and lax.ppermute only.
A program may use at most 128 MiB of HBM per device.

v0:
```python
import functools
import math

import jax
import jax.numpy as jnp
from jax import lax
from jax.experimental import pallas as pl
from jax.experimental.pallas import tpu as pltpu
from jax.sharding import Mesh, PartitionSpec as P

QD, LQ, PD, LP, E, D = 8, 32, 4, 128, 128, 4096
QT, PT = QD * LQ, PD * LP
NEG, CANDS, NEAR = 16, 144, 128
GROUPS, QUERIES = 8, 2048
POOL = GROUPS * PD
PROWS, QROWS = PT + 16, QT + 48
QB, PB = 4, 8
LANES = QB * QD
DIVISOR = 0.05
SCALE = math.log2(math.e) / DIVISOR
EPS = 1e-6
HI = lax.Precision.HIGHEST
f32, bf16, i32 = jnp.float32, jnp.bfloat16, jnp.int32
AXES = ("yh", "x", "a", "b", "yl", "c")
GROUP = ("yh", "x")
VMEM = pl.BlockSpec(memory_space=pltpu.VMEM)
SMEM = pl.BlockSpec(memory_space=pltpu.SMEM)
ANY = pl.BlockSpec(memory_space=pl.ANY)
MIB = 1024 * 1024
LIMIT = 24
COLS = 1024
DEAD = -1e4


def sds(shape, dtype):
    return jax.ShapeDtypeStruct(shape, dtype)


def iota(shape, axis):
    return lax.broadcasted_iota(i32, shape, axis)


def nt(x, y, **kw):
    return lax.dot_general(x, y, (((1,), (1,)), ((), ())), preferred_element_type=f32, **kw)


def tn(x, y, **kw):
    return lax.dot_general(x, y, (((0,), (0,)), ((), ())), preferred_element_type=f32, **kw)


def nn(x, y, **kw):
    return jnp.dot(x, y, preferred_element_type=f32, **kw)


def pieces(x):
    hi = x.astype(bf16)
    mid = (x - hi.astype(f32)).astype(bf16)
    low = (x - hi.astype(f32) - mid.astype(f32)).astype(bf16)
    return hi, mid, low


def unit_raw(raw):
    return raw / jnp.sqrt(jnp.sum(raw * raw, axis=-1, keepdims=True) + EPS)


def back(raw, up):
    length = jnp.sqrt(jnp.sum(raw * raw, axis=-1, keepdims=True) + EPS)
    direct = raw / length
    return (up - direct * jnp.sum(direct * up, axis=-1, keepdims=True)) / length


def live_rows(len_ref, first, rows):
    row = iota((rows, E), 0)
    lens = jnp.zeros((rows, E), i32)
    for k in range(rows // LP):
        lens = jnp.where(row // LP == k, len_ref[first + k], lens)
    return row % LP < lens


def project(
    q_len_ref, p_len_ref, count_ref, x_q_hbm, x_p_hbm, w_hbm, teacher_hbm, ids_hbm,
    raw_ref, p_ref, near_ref, far_ref, const_ref,
    x_q_ref, x_p_ref, w_ref, teacher_ref, ids_ref, sems,
):
    half = PT // 2
    moves = [
        (teacher_hbm, teacher_ref),
        (ids_hbm, ids_ref),
        (w_hbm, w_ref),
        (x_p_hbm.at[:half], x_p_ref.at[:half]),
        (x_p_hbm.at[half:], x_p_ref.at[half:]),
        (x_q_hbm, x_q_ref),
    ]
    copies = [pltpu.make_async_copy(a, b, sems.at[k]) for k, (a, b) in enumerate(moves)]
    for copy in copies:
        copy.start()
    lane, row = iota((16, E), 1), iota((16, E), 0)
    q = row * 4 + lane // LQ
    q_lens, p_lens = jnp.zeros((16, E), i32), jnp.zeros((16, E), i32)
    for k in range(QD):
        q_lens = jnp.where(q == k, q_len_ref[k], q_lens)
    for k in range(PD):
        p_lens = jnp.where(row == k, p_len_ref[k], p_lens)
    flags = (lane % LQ < q_lens).astype(f32).astype(bf16)
    near_ref[QT : QT + 16, :] = flags
    far_ref[QT : QT + 16, :] = flags
    p_ref[PT:PROWS, :] = p_lens.astype(f32).astype(bf16)
    copies[0].wait()
    copies[1].wait()
    teacher = teacher_ref[...]
    count = jnp.zeros((QD, CANDS), i32)
    for k in range(QD):
        count = jnp.where(iota((QD, CANDS), 0) == k, count_ref[k], count)
    live = iota((QD, CANDS), 1) < NEAR + count
    masked = jnp.where(live, teacher, -1e30)
    top = jnp.max(masked, axis=1, keepdims=True)
    lse = top + jnp.log(jnp.sum(jnp.exp(masked - top), axis=1, keepdims=True))
    put_pieces(near_ref, teacher[:, :NEAR] - lse, jnp.zeros((QD, E), f32))
    far = teacher[:, NEAR:] - lse
    far_live = (iota((QD, NEG), 1) < count[:, :NEG]).astype(f32)
    far_prob = jnp.exp(far) * far_live
    const_ref[...] = jnp.full((8, E), jnp.sum(far_prob * jnp.where(far_live > 0, far, 0.0)))
    ids = ids_ref[...]
    slot = (ids >> 7) * PD + (ids & (PD - 1))
    pool = iota((QD, E), 1)
    number, prob = jnp.zeros((QD, E), f32), jnp.zeros((QD, E), f32)
    for k in range(NEG):
        hit = slot[:, k : k + 1] == pool
        number = number + jnp.where(hit, far_live[:, k : k + 1], 0.0)
        prob = prob + jnp.where(hit, far_prob[:, k : k + 1], 0.0)
    put_pieces(far_ref, prob, number)
    copies[2].wait()
    w = w_ref[...]
    for k in range(2):
        copies[3 + k].wait()
        at = slice(k * half, (k + 1) * half)
        raw = nn(x_p_ref[at, :], w)
        raw_ref[at, :] = raw
        p_ref[at, :] = jnp.where(live_rows(p_len_ref, 2 * k, half), unit_raw(raw), 0.0).astype(bf16)
    copies[5].wait()
    raw = nn(x_q_ref[...], w)
    raw_ref[PT:, :] = raw
    vecs = unit_raw(raw).astype(bf16)
    near_ref[:QT, :] = vecs
    far_ref[:QT, :] = vecs


def put_pieces(ref, value, other):
    hi, mid, low = (v.astype(f32) for v in pieces(value))
    ref[QT + 16 : QT + 32, :] = jnp.concatenate([hi, mid]).astype(bf16)
    ref[QT + 32 : QT + 48, :] = jnp.concatenate([low, other]).astype(bf16)


def with_bias(p_ref):
    lens = p_ref[PT:PROWS, :].astype(f32)[:PD]
    live = iota((PD, LP, E), 1).astype(f32) < lens[:, None, :]
    bias = jnp.where(live.reshape(PT, E) | (iota((PT, E), 1) > 0), 0.0, DEAD).astype(bf16)
    return jnp.concatenate([p_ref[:PT, :], bias], axis=1)


def flags_of(q_ref):
    rows = q_ref[QT : QT + 16, :].astype(f32)
    return jnp.concatenate([rows[0:1], rows[1:2]], axis=1)


def lane_of(at, block):
    return (at ^ block) * QD


def spread(at, block):
    return (iota((QT, LANES), 1) == lane_of(at, block) + iota((QT, LANES), 0) // LQ).astype(f32)


def columns_to_lanes(q_refs, at, column):
    n = column.shape[0]
    pick = (iota((n, E), 1) == column).astype(f32).astype(bf16)
    value, exact = jnp.zeros((n, LANES), f32), jnp.zeros((n, LANES), f32)
    for block in range(QB):
        got = nt(pick, q_refs[block][QT + 16 : QT + 48, :])
        lane, row = iota((32, LANES), 1), iota((32, LANES), 0)
        there = lane == lane_of(at, block) + row % QD
        value = value + nn(got, (there & (row < 24)).astype(f32), precision=HI)
        exact = exact + nn(got, (there & (row >= 24)).astype(f32), precision=HI)
    return value, exact


def far_columns(pos_ref, yh):
    row = iota((2 * PD, E), 0)
    at_yh = jnp.where(row // PD == 1, 1 - yh, yh)
    return (at_yh * 4 + pos_ref[0]) * PD + row % PD


def near_columns(pos_ref):
    row = iota((PB * PD, E), 0)
    block, p = row // PD, row % PD

    def at(k, bit):
        return jnp.where((block >> bit) & 1 == 1, 1 - pos_ref[k], pos_ref[k])

    return (((pos_ref[1] * 2 + at(2, 1)) * 2 + at(3, 0)) * 2 + at(4, 2)) * PD + p


def block_scores(at, q_refs, p_refs, w_ref, tot_ref, wide_ref):
    one = (iota((QT, E), 1) == 0).astype(f32).astype(bf16)
    for qb in range(QB):
        wide_ref[qb * QT : (qb + 1) * QT, :E] = q_refs[qb][:QT, :]
        wide_ref[qb * QT : (qb + 1) * QT, E:] = one
    for pb, p_ref in enumerate(p_refs):
        p = with_bias(p_ref)
        for qb in range(QB):
            at_q = slice(qb * QT, (qb + 1) * QT)
            w = jnp.exp2(nt(p, wide_ref[at_q, :]) * SCALE)
            tot_ref[pb * PD : (pb + 1) * PD, at_q] = jnp.sum(w.reshape(PD, LP, QT), axis=1)
            w_ref[pb, :, at_q] = w
    scores = jnp.zeros((len(p_refs) * PD, LANES), f32)
    for qb in range(QB):
        logs = DIVISOR * jnp.log(tot_ref[:, qb * QT : (qb + 1) * QT]) * flags_of(q_refs[qb])
        scores = scores + nn(logs, spread(at, qb), precision=HI)
    return scores


def forward_first(pos_ref, *refs):
    near_q, p_refs, (w_ref, tot_ref, scores_ref, wide_ref) = split(refs, "q", PB // 2, 4)
    scores_ref[...] = block_scores(pos_ref[1], near_q, p_refs, w_ref, tot_ref, wide_ref)


def forward_second(pos_ref, scores_ref, *refs):
    near_q, far_q, p_refs, far_p, outs = split(refs, "q", "q", PB // 2, 2, 8)
    (w_ref, tot_ref, more_ref, far_w_ref, far_tot_ref, info_ref, row_ref, wide_ref) = outs
    near = block_scores(pos_ref[1], near_q, p_refs, w_ref, tot_ref, wide_ref)
    far = block_scores(pos_ref[0], far_q, far_p, far_w_ref, far_tot_ref, wide_ref)
    prob, number = columns_to_lanes(far_q, pos_ref[0], far_columns(pos_ref, pos_ref[5]))
    more_ref[...] = near
    info_ref[0] = prob
    info_ref[1] = number
    info_ref[2] = far
    near = jnp.sum(jnp.exp(scores_ref[...]) + jnp.exp(near), axis=0, keepdims=True)
    far = jnp.sum(number * jnp.exp(far), axis=0, keepdims=True)
    both = jnp.concatenate([near, far, jnp.zeros((6, LANES), f32)], axis=0)
    both = jnp.concatenate([both, jnp.zeros((8, E - LANES), f32)], axis=1)
    for k in range(16):
        row_ref[k] = both


def split(refs, *sizes):
    out, k = [], 0
    for n in sizes:
        group = list(refs[k : k + (3 if n == "q" else n)])
        k += len(group)
        if n == "q":
            group = group[:2] + [group[2].at[0], group[2].at[1]]
        out.append(group)
    return out


def chosen(rows, base):
    pick = (iota((LANES, LANES), 0) == base + iota((LANES, LANES), 1) % QD).astype(f32)
    got = nn(rows, pick, precision=HI)
    keep = iota((4, LANES), 1) // QD == iota((4, LANES), 0)
    return jnp.sum(jnp.where(keep, got, 0.0), axis=0, keepdims=True)


def coefficients(at, q_refs, grad, tot_ref, out_ref):
    for qb in range(QB):
        at_q = slice(qb * QT, (qb + 1) * QT)
        spread_grad = nt(grad, spread(at, qb), precision=HI)
        out_ref[:, at_q] = spread_grad * flags_of(q_refs[qb]) / tot_ref[:, at_q]


def block_grads(q_refs, p_refs, w_ref, coef_ref, put_p, g_ref, q_ref, q_grad):
    for qb in range(QB):
        q_ref[qb * QT : (qb + 1) * QT, :] = q_refs[qb][:QT, :]
    for pb, p_ref in enumerate(p_refs):
        for k in range(PD):
            at_p = slice(k * LP, (k + 1) * LP)
            row = coef_ref[pb * PD + k : pb * PD + k + 1, :]
            g_ref[at_p, :] = (w_ref[pb, at_p, :] * row).astype(bf16)
        put_p(pb, nn(g_ref[...], q_ref[...]))
        q_grad = q_grad + tn(p_ref[:PT, :], g_ref[...])
    return q_grad


def backward_first(pos_ref, const_ref, rows_ref, scores_ref, more_ref, tot_ref, more_tot_ref, far_tot_ref,
                   info_ref, *refs):
    near_q, far_q, p_refs, (w_ref,), outs = split(refs, "q", "q", PB // 2, 1, 8)
    (p_send, q_part, coef_ref, far_coef_ref, loss_ref, more_coef_ref, g_ref, q_ref) = outs
    x, a = pos_ref[0], pos_ref[1]
    by_x = [sum(rows_ref[4 * i + j, 0:1, :LANES] for j in range(4)) for i in range(4)]
    by_a = [sum(rows_ref[4 * i + j, 1:2, :LANES] for i in range(4)) for j in range(4)]
    by_x, by_a = jnp.concatenate(by_x, axis=0), jnp.concatenate(by_a, axis=0)
    own_x = (iota((4, LANES), 0) == x).astype(f32)
    own_a = (iota((4, LANES), 0) == a).astype(f32)
    lse = jnp.log(jnp.sum(by_x * own_x, axis=0, keepdims=True) + chosen(by_a, x * QD))
    far_lse = jnp.log(jnp.sum(by_a * own_a, axis=0, keepdims=True) + chosen(by_x, a * QD))

    target, _ = columns_to_lanes(near_q, a, near_columns(pos_ref))
    student = jnp.concatenate([scores_ref[...], more_ref[...]], axis=0) - lse
    prob = jnp.exp(target)
    near_grad = (jnp.exp(student) - prob) / QUERIES
    loss = jnp.sum(prob * (target - student))
    far_prob, number = info_ref[0], info_ref[1]
    far_student = jnp.where(number > 0, info_ref[2] - far_lse, 0.0)
    far_grad = (number * jnp.exp(far_student) - far_prob) / QUERIES
    loss = loss + const_ref[0, 0] - jnp.sum(far_prob * far_student)
    loss_ref[...] = jnp.full((8, E), loss)
    half = PB * PD // 2
    coefficients(a, near_q, near_grad[half:], more_tot_ref, more_coef_ref)
    coefficients(a, near_q, near_grad[:half], tot_ref, coef_ref)
    coefficients(x, far_q, far_grad, far_tot_ref, far_coef_ref)

    def put(pb, value):
        p_send[pb] = value.astype(bf16)

    zero = jnp.zeros((E, QB * QT), f32)
    q_part[...] = block_grads(near_q, p_refs, w_ref, more_coef_ref, put, g_ref, q_ref, zero)


def backward_second(coef_ref, far_coef_ref, q_part, *refs):
    near_q, far_q, p_refs, far_p, (w_ref, far_w_ref), outs = split(refs, "q", "q", PB // 2, 2, 2, 7)
    (q_keep, near_send, far_send, p_keep, p_yh, g_ref, q_ref) = outs

    def near_put(pb, value):
        p_keep[pb] = value

    def far_put(pb, value):
        if pb == 0:
            p_keep[0] = p_keep[0] + value
        else:
            p_yh[...] = value.astype(bf16)

    q_grad = block_grads(near_q, p_refs, w_ref, coef_ref, near_put, g_ref, q_ref, q_part[...]).T
    zero = jnp.zeros((E, QB * QT), f32)
    far_q_grad = block_grads(far_q, far_p, far_w_ref, far_coef_ref, far_put, g_ref, q_ref, zero).T
    q_keep[0] = q_grad[:QT] + far_q_grad[:QT]
    q_keep[1] = q_grad[QT : 2 * QT]
    q_keep[2] = far_q_grad[QT : 2 * QT]
    for k in range(2):
        near_send[k] = q_grad[(2 + k) * QT : (3 + k) * QT].astype(bf16)
        far_send[k] = far_q_grad[(2 + k) * QT : (3 + k) * QT].astype(bf16)


def merge_passages(keep_ref, more_ref, *outs):
    for k in range(4):
        outs[k][...] = (keep_ref[k] + more_ref[k].astype(f32)).astype(outs[k].dtype)


def merge_queries(keep_ref, near_ref, far_ref, own_ref, near_out, far_out):
    own_ref[...] = keep_ref[0] + near_ref[0].astype(f32) + far_ref[0].astype(f32)
    near_out[...] = (keep_ref[1] + near_ref[1].astype(f32)).astype(bf16)
    far_out[...] = (keep_ref[2] + far_ref[1].astype(f32)).astype(bf16)


def finish(pos_ref, p_len_ref, x_q_ref, x_p_ref, loss_ref, raw_ref, q_own, p_own, *refs):
    q_in, p_in = refs[:2], refs[2:6]
    out_ref, backs_ref = refs[6:]
    i = pl.program_id(0)

    @pl.when(i == 0)
    def _():
        q_grad = q_own[...] + sum(r[...].astype(f32) for r in q_in)
        p_grad = p_own[...] + sum(r[...].astype(f32) for r in p_in)
        p_grad = jnp.where(live_rows(p_len_ref, 0, PT), p_grad, 0.0)
        backs_ref[:, :QT] = back(raw_ref[PT:, :], q_grad).T.astype(bf16)
        backs_ref[:, QT:] = back(raw_ref[:PT, :], p_grad).T.astype(bf16)

    grad_block(x_q_ref, x_p_ref, loss_ref, backs_ref, out_ref, 0)


def finish_more(pos_ref, x_q_ref, x_p_ref, loss_ref, backs_ref, out_ref):
    grad_block(x_q_ref, x_p_ref, loss_ref, backs_ref, out_ref, 8)


def grad_block(x_q_ref, x_p_ref, loss_ref, backs_ref, out_ref, lane):
    grad = nn(backs_ref[:, :QT], x_q_ref[...]) + nn(backs_ref[:, QT:], x_p_ref[...])
    hi, mid, low = (
        jnp.concatenate([v.astype(f32)] * 2, axis=0) for v in pieces(loss_ref[0:8, :])
    )
    at = iota((16, E), 1)
    rows = jnp.where(at == lane, hi, 0.0)
    rows = jnp.where(at == lane + 1, mid, rows)
    rows = jnp.where(at == lane + 2, low, rows)
    for k in range(COLS // 128):
        out_ref[k, :128, :] = grad[:, k * 128 : (k + 1) * 128].astype(bf16)
        out_ref[k, 128:, :] = rows.astype(bf16)


def sum_rows(n, x_ref, out_ref):
    total = x_ref[0].astype(f32)
    for k in range(1, n):
        total = total + x_ref[k].astype(f32)
    body = total[:128].astype(bf16)
    loss = jnp.sum(total[128:129, :], axis=1, keepdims=True)
    hi, mid, low = (v.astype(f32) for v in pieces(jnp.broadcast_to(loss, (16, E))))
    at = iota((16, E), 1)
    rows = jnp.where(at == 0, hi, jnp.where(at == 1, mid, jnp.where(at == 2, low, 0.0))).astype(bf16)
    for k in range(8):
        out_ref[k, :128, :] = body
        out_ref[k, 128:, :] = rows


def sum_last(n, x_ref, out_ref, loss_ref):
    total = x_ref[0].astype(f32)
    for k in range(1, n):
        total = total + x_ref[k].astype(f32)
    body = total[:128].T.astype(bf16)
    for k in range(16):
        out_ref[k] = body
    loss = jnp.sum(total[128:129, :], axis=1, keepdims=True)
    loss_ref[...] = jnp.broadcast_to(loss, (8, E)) / QUERIES


def call(kernel, out_shape, n_in, smem=(0,), scratch=(), name=None):
    return pl.pallas_call(
        kernel,
        out_shape=out_shape,
        in_specs=[SMEM if k in smem else VMEM for k in range(n_in)],
        out_specs=jax.tree.map(lambda _: VMEM, out_shape),
        scratch_shapes=list(scratch),
        compiler_params=pltpu.CompilerParams(vmem_limit_bytes=LIMIT * MIB),
        name=name,
    )


def flip(x, axis):
    return lax.ppermute(x, axis, [(0, 1), (1, 0)])


def flip2(x):
    return lax.ppermute(x, ("b", "yl"), [(i, i ^ 3) for i in range(4)])


def swap(x, axis, d):
    return lax.ppermute(x, axis, [(i, i ^ d) for i in range(4)])


def doubled(x, axis):
    other = swap(x, axis, 1)
    return [x, other, swap(jnp.stack([x, other]), axis, 2)]


def local(x_q, x_p, w, query_len, passage_len, neg_ids, neg_count, teacher):
    x_q, x_p = x_q.reshape(QT, D), x_p.reshape(PT, D)
    c = lax.axis_index("c")
    pos = jnp.stack([lax.axis_index(n) for n in ("x", "a", "b", "yl", "c", "yh")]).astype(i32)

    raw, p, near, far, const = pl.pallas_call(
        project,
        in_specs=[SMEM] * 3 + [ANY] * 5,
        out_specs=[VMEM] * 5,
        out_shape=[sds((PT + QT, E), f32), sds((PROWS, E), bf16), sds((QROWS, E), bf16),
                   sds((QROWS, E), bf16), sds((8, E), f32)],
        scratch_shapes=[
            pltpu.VMEM((QT, D), bf16), pltpu.VMEM((PT, D), bf16), pltpu.VMEM((D, E), bf16),
            pltpu.VMEM((QD, CANDS), f32), pltpu.VMEM((QD, NEG), i32), pltpu.SemaphoreType.DMA((6,)),
        ],
        compiler_params=pltpu.CompilerParams(vmem_limit_bytes=60 * MIB),
        name="project",
    )(query_len, passage_len, neg_count, x_q, x_p, w, teacher, neg_ids)

    ps = [p, flip(p, "yl"), flip(p, "b"), flip2(p)]
    ps = ps + [flip(v, "c") for v in ps]
    yh_p = flip(p, "yh")
    near_q, far_q = doubled(near, "a"), doubled(far, "x")
    wide = [pltpu.VMEM((QB * QT, 2 * E), bf16)]
    half, tokens = PB * PD // 2, QB * QT
    near_ps, more_ps, far_ps = ps[:4], ps[4:], [p, yh_p]
    w_near, tot, scores = call(
        forward_first,
        [sds((4, PT, tokens), f32), sds((half, tokens), f32), sds((half, LANES), f32)],
        8, scratch=wide, name="forward_first",
    )(pos, *near_q, *near_ps)
    w_more, more_tot, more, w_far, far_tot, info, rows = call(
        forward_second,
        [sds((4, PT, tokens), f32), sds((half, tokens), f32), sds((half, LANES), f32),
         sds((2, PT, tokens), f32), sds((2 * PD, tokens), f32), sds((3, 2 * PD, LANES), f32),
         sds((16, 8, E), f32)],
        14, scratch=wide, name="forward_second",
    )(pos, scores, *near_q, *far_q, *more_ps, *far_ps)
    rows = lax.all_to_all(rows, ("x", "a"), 0, 0, tiled=True)
    room = [pltpu.VMEM((PT, tokens), bf16), pltpu.VMEM((tokens, E), bf16)]
    p_send, q_part, coef, far_coef, loss = call(
        backward_first,
        [sds((4, PT, E), bf16), sds((E, tokens), f32), sds((half, tokens), f32),
         sds((2 * PD, tokens), f32), sds((8, E), f32)],
        20, scratch=[pltpu.VMEM((half, tokens), f32)] + room, name="backward_first",
    )(pos, const, rows, scores, more, tot, more_tot, far_tot, info, *near_q, *far_q, *more_ps, w_more)
    p_more = flip(p_send, "c")
    q_keep, near_send, far_send, p_keep, p_yh = call(
        backward_second,
        [sds((3, QT, E), f32), sds((2, QT, E), bf16), sds((2, QT, E), bf16), sds((4, PT, E), f32),
         sds((PT, E), bf16)],
        17, smem=(), scratch=room, name="backward_second",
    )(coef, far_coef, q_part, *near_q, *far_q, *near_ps, *far_ps, w_near, w_far)

    near_in, far_in = swap(near_send, "a", 2), swap(far_send, "x", 2)
    p_own, p1, p2, p3 = call(
        merge_passages, [sds((PT, E), f32)] + [sds((PT, E), bf16)] * 3, 2, smem=(), name="merge_passages"
    )(p_keep, p_more)
    p_in = [flip(p1, "yl"), flip(p2, "b"), flip2(p3), flip(p_yh, "yh")]
    q_own, near_send, far_send = call(
        merge_queries, [sds((QT, E), f32)] + [sds((QT, E), bf16)] * 2, 3, smem=(), name="merge_queries"
    )(q_keep, near_in, far_in)
    q_in = [swap(near_send, "a", 1), swap(far_send, "x", 1)]

    def whole(shape):
        return pl.BlockSpec(shape, lambda i, pos: (0,) * len(shape))

    def columns(rows, half):
        return pl.BlockSpec((rows, COLS), lambda i, pos: (0, half(pos) * (D // 2 // COLS) + i))

    def halves(kernel, half, extra, ins, outs, out_shape, name):
        return pl.pallas_call(
            kernel,
            grid_spec=pltpu.PrefetchScalarGridSpec(
                num_scalar_prefetch=1,
                grid=(D // 2 // COLS,),
                in_specs=extra + [columns(QT, half), columns(PT, half)] + [whole(s) for s in ins],
                out_specs=[pl.BlockSpec((COLS // 128, 144, E), lambda i, pos: (i, 0, 0))]
                + [whole(s) for s in outs],
            ),
            out_shape=[sds((16, 144, E), bf16)] + out_shape,
            compiler_params=pltpu.CompilerParams(vmem_limit_bytes=LIMIT * MIB),
            name=name,
        )

    operands = [loss, raw, q_own, p_own, *q_in, *p_in]
    send, backs = halves(
        finish, lambda pos: 1 - pos[4], [SMEM], [v.shape for v in operands], [(E, QT + PT)],
        [sds((E, QT + PT), bf16)], "finish",
    )(pos, passage_len, x_q, x_p, *operands)
    other = flip(send, "c")
    (mine,) = halves(
        finish_more, lambda pos: pos[4], [], [loss.shape, backs.shape], [], [], "finish_more"
    )(pos, x_q, x_p, loss, backs)

    part = (mine.astype(f32) + other.astype(f32)).astype(bf16)
    part = lax.all_to_all(part, ("yh", "x", "yl"), 0, 0, tiled=True)
    part = call(functools.partial(sum_rows, 16), sds((8, 144, E), bf16), 1, smem=(), name="sum_rows")(part)
    part = lax.all_to_all(part, ("a", "b"), 0, 0, tiled=True)
    part, total = call(
        functools.partial(sum_last, 8), [sds((16, 128, E), bf16), sds((8, E), f32)], 1, smem=(),
        name="sum_last",
    )(part)
    part = lax.all_to_all(part, ("yh", "x", "yl"), 0, 0, tiled=True)
    other = flip(part, "c")
    first = jnp.where(c == 0, part, other)
    second = jnp.where(c == 0, other, part)
    grad = jnp.concatenate([first, second]).astype(f32).reshape(D, E)
    return grad, total[0, 0]


def solution(mesh):
    wide = Mesh(mesh.devices.reshape(2, 4, 4, 2, 2, 2), AXES)
    return jax.shard_map(
        local,
        mesh=wide,
        in_specs=(
            P(AXES, None, None),
            P(AXES, None, None),
            P(),
            P(AXES),
            P(AXES),
            P(AXES, None),
            P(AXES),
            P(AXES, None),
        ),
        out_specs=(P(), P()),
        check_vma=False,
    )
```

profile of v0, /device:TPU:1, one launch (start us, length us, event | category | flops | bytes accessed | tf_op | source)
XLA Modules:
  0.0 142.1 jit_solution(14010488155465463455)
XLA Ops:
  0.6 5.7 %project.1 = (f32[768,128]{1,0:T(8,128)}, bf16[528,128]{1,0:T(8,128)(2,1)}, bf16[304,128]{1,0:T(8,128)(2,1)}, bf16[304,128]{1,0:T(8,128)(2,1)}, f32[8,128]{1,0:T(8,128)}) custom-call(s32[8]{0:T(128)} %q_len_ref.1, s32[4]{0:T(128)} %p_len_ref.3, s32[8]{0:T(128)} %count_ref.1, bf16[256,4096]{1,0:T(8,128)(2,1)} %bitcast.19, bf16[512,4096]{1,0:T(8,128)(2,1)} %bitcast.16, ...), custom_call_target="tpu_custom_call" | custom-call | tf_op jit(solution)/shard_map/project/pallas_call | solution.py:446
  6.4 3.9 %collective-permute-start = (bf16[304,128]{1,0:T(8,128)(2,1)}, bf16[304,128]{1,0:T(8,128)(2,1)S(1)}, u32[]{:S(2)}, u32[]{:S(2)}) collective-permute-start(bf16[304,128]{1,0:T(8,128)(2,1)} %get-tuple-element.39.refs_0_), channel_id=1, source_target_pairs={{0,8},{8,0},{16,24},{24,16},{1,9},{9,1},{17,25},{25,17},{2,10},{10... | collective-permute-start | bytes 233480 | tf_op jit(solution)/shard_map/ppermute | solution.py:433
  10.3 1.2 collective-permute-start.5
  11.5 2.9 %collective-permute-start.11 = (bf16[528,128]{1,0:T(8,128)(2,1)}, bf16[528,128]{1,0:T(8,128)(2,1)S(1)}, u32[]{:S(2)}, u32[]{:S(2)}) collective-permute-start(bf16[528,128]{1,0:T(8,128)(2,1)} %get-tuple-element.40.refs_3_.refs_10_.refs_6_), channel_id=1, source_target_pairs={{0,128},{128,0},{1,129},{129,1},{2,130},{130,2},{3,131},{131,3},{4... | collective-permute-start | bytes 405512 | tf_op jit(solution)/shard_map/ppermute | solution.py:425
  14.4 0.9 pad_maximum_fusion.1
  15.3 6.5 %collective-permute-start.1 = (bf16[2,304,128]{2,1,0:T(8,128)(2,1)S(1)}, bf16[2,304,128]{2,1,0:T(8,128)(2,1)S(1)}, u32[]{:S(2)}, u32[]{:S(2)}) collective-permute-start(bf16[2,304,128]{2,1,0:T(8,128)(2,1)S(1)} %pad_maximum_fusion.1), channel_id=1, source_target_pairs={{0,16},{8,24},{16,0},{24,8},{1,17},{9,25},{17,1},{25,9},{2,18},{10... | collective-permute-start | bytes 466952 | tf_op jit(solution)/shard_map/ppermute | solution.py:433
  21.8 2.5 %collective-permute-start.3 = (bf16[528,128]{1,0:T(8,128)(2,1)}, bf16[528,128]{1,0:T(8,128)(2,1)S(1)}, u32[]{:S(2)}, u32[]{:S(2)}) collective-permute-start(bf16[528,128]{1,0:T(8,128)(2,1)} %get-tuple-element.40.refs_3_.refs_10_.refs_6_), channel_id=1, source_target_pairs={{0,4},{4,0},{1,5},{5,1},{2,6},{6,2},{3,7},{7,3},{8,12},{12,8},{9,1... | collective-permute-start | bytes 405512 | tf_op jit(solution)/shard_map/ppermute | solution.py:425
  25.4 2.8 %collective-permute-start.6 = (bf16[2,304,128]{2,1,0:T(8,128)(2,1)S(1)}, bf16[2,304,128]{2,1,0:T(8,128)(2,1)S(1)}, u32[]{:S(2)}, u32[]{:S(2)}) collective-permute-start(bf16[2,304,128]{2,1,0:T(8,128)(2,1)S(1)} %pad_maximum_fusion.2), channel_id=1, source_target_pairs={{0,64},{32,96},{64,0},{96,32},{1,65},{33,97},{65,1},{97,33},{2,66}... | collective-permute-start | bytes 466952 | tf_op jit(solution)/shard_map/ppermute | solution.py:433
  28.2 3.6 %collective-permute-done.4.refs_6_.refs_9_ = bf16[528,128]{1,0:T(8,128)(2,1)S(1)} collective-permute-done((bf16[528,128]{1,0:T(8,128)(2,1)}, bf16[528,128]{1,0:T(8,128)(2,1)S(1)}, u32[]{:S(2)}, u32[]{:S(2)}) %collective-permute-start.4) | collective-permute-done | bytes 135200 | tf_op jit(solution)/shard_map/ppermute | solution.py:429
  31.8 2.3 %collective-permute-start.7 = (bf16[528,128]{1,0:T(8,128)(2,1)}, bf16[528,128]{1,0:T(8,128)(2,1)S(1)}, u32[]{:S(2)}, u32[]{:S(2)}) collective-permute-start(bf16[528,128]{1,0:T(8,128)(2,1)} %get-tuple-element.40.refs_3_.refs_10_.refs_6_), channel_id=1, source_target_pairs={{0,1},{1,0},{2,3},{3,2},{4,5},{5,4},{6,7},{7,6},{8,9},{9,8},{10,11... | collective-permute-start | bytes 405512 | tf_op jit(solution)/shard_map/ppermute | solution.py:425
  34.3 1.4 collective-permute-start.10
  36.3 0.9 copy-done.2
  38.1 2.3 %forward_first.1 = (f32[4,512,1024]{2,1,0:T(8,128)S(1)}, f32[16,1024]{1,0:T(8,128)S(1)}, f32[16,32]{1,0:T(8,128)S(1)}) custom-call(s32[6]{0:T(128)S(1)} %stack.45.pos_ref, bf16[304,128]{1,0:T(8,128)(2,1)S(1)} %copy-done.4, bf16[304,128]{1,0:T(8,128)(2,1)S(1)} %collective-permute-done.refs_1_, bf16[2,304,128]{2,1,0:T(8,128)(2,1)S(1)} %collective-permute-done.1.refs_2_, ...), custom_call_target="tpu_custom_call" | custom-call | tf_op jit(solution)/shard_map/forward_first/pallas_call | solution.py:467
  41.3 3.9 %forward_second.1 = (f32[4,512,1024]{2,1,0:T(8,128)S(1)}, f32[16,1024]{1,0:T(8,128)S(1)}, f32[16,32]{1,0:T(8,128)S(1)}, f32[2,512,1024]{2,1,0:T(8,128)S(1)}, f32...) custom-call(s32[6]{0:T(128)S(1)} %stack.45.pos_ref, ...), custom_call_target="tpu_custom_call" | custom-call | tf_op jit(solution)/shard_map/forward_second/pallas_call | solution.py:472
  45.2 13.9 %all_to_all.20.rows_ref = f32[16,8,128]{2,1,0:T(8,128)S(1)} all-to-all(f32[16,8,128]{2,1,0:T(8,128)S(1)} %get-tuple-element.43), channel_id=1, replica_groups=mesh['yh'=2,'x'=4,'a'=4,'b'=2,'yl'=2,'c'=2] {'x','a'}, dimensions={0} | all-to-all | bytes 131072 | tf_op jit(solution)/shard_map/all_to_all | solution.py:479
  59.1 4.1 %backward_first.1 = (bf16[4,512,128]{2,1,0:T(8,128)(2,1)S(1)}, f32[128,1024]{1,0:T(8,128)S(1)}, f32[16,1024]{1,0:T(8,128)S(1)}, f32[8,1024]{1,0:T(8,128)S(1)}, f32[8,128]{1,0:T(8,128)S(1)}) custom-call(s32[6]{0:T(128)S(1)} %stack.45.pos_ref, f32[8,128]{1,0:T(8,128)S(1)} %copy-done.8, f32[16,8,128]{2,1,0:T(8,128)S(1)} %all_to_all.20.rows_ref, ...), custom_call_target="tpu_custom_call" | custom-call | tf_op jit(solution)/shard_map/backward_first/pallas_call | solution.py:481
  63.2 1.6 %collective-permute-start.14 = (bf16[4,512,128]{2,1,0:T(8,128)(2,1)S(1)}, bf16[4,512,128]{2,1,0:T(8,128)(2,1)S(1)}, u32[]{:S(2)}, u32[]{:S(2)}) collective-permute-start(bf16[4,512,128]{2,1,0:T(8,128)(2,1)S(1)} %get-tuple-element.62), channel_id=1, source_target_pairs={{0,1},{1,0},{2,3},{3,2},{4,5},{5,4},{6,7},{7,6},{8,9},{9,8},{10,11... | collective-permute-start | bytes 1572872 | tf_op jit(solution)/shard_map/ppermute | solution.py:425
  64.9 2.8 %backward_second.1 = (f32[3,256,128]{2,1,0:T(8,128)S(1)}, bf16[2,256,128]{2,1,0:T(8,128)(2,1)S(1)}, bf16[2,256,128]{2,1,0:T(8,128)(2,1)S(1)}, f32[4,512,128]{2,1,0:T(8,128)S(1)}, bf16[512,128]{1,0:T(8,128)(2,1)S(1)}) custom-call(f32[16,1024]{1,0:T(8,128)S(1)} %get-tuple-element.52.coef_ref, f32[8,1024]{1,0:T(8,128)S(1)} %get-tuple-element.53.far_coef_ref, ...), custom_call_target="tpu_custom_call" | custom-call | tf_op jit(solution)/shard_map/backward_second/pallas_call | solution.py:488
  68.3 0.9 collective-permute-start.13
  69.3 2.9 %collective-permute-start.20 = (bf16[512,128]{1,0:T(8,128)(2,1)S(1)}, bf16[512,128]{1,0:T(8,128)(2,1)S(1)}, u32[]{:S(2)}, u32[]{:S(2)}) collective-permute-start(bf16[512,128]{1,0:T(8,128)(2,1)S(1)} %get-tuple-element.69), channel_id=1, source_target_pairs={{0,128},{128,0},{1,129},{129,1},{2,130},{130,2},{3,131},{131,3},{4... | collective-permute-start | bytes 393224 | tf_op jit(solution)/shard_map/ppermute | solution.py:425
  73.4 3.7 %collective-permute-done.12.near_ref = bf16[2,256,128]{2,1,0:T(8,128)(2,1)S(1)} collective-permute-done((bf16[2,256,128]{2,1,0:T(8,128)(2,1)S(1)}, bf16[2,256,128]{2,1,0:T(8,128)(2,1)S(1)}, u32[]{:S(2)}, u32[]{:S(2)}) %collective-permute-start.12) | collective-permute-done | bytes 131104 | tf_op jit(solution)/shard_map/ppermute | solution.py:433
  77.1 4.3 %collective-permute-start.19 = (bf16[512,128]{1,0:T(8,128)(2,1)S(1)}, bf16[512,128]{1,0:T(8,128)(2,1)S(1)}, u32[]{:S(2)}, u32[]{:S(2)}) collective-permute-start(bf16[512,128]{1,0:T(8,128)(2,1)S(1)} %get-tuple-element.68), channel_id=1, source_target_pairs={{0,6},{2,4},{4,2},{6,0},{1,7},{3,5},{5,3},{7,1},{8,14},{10,12},{12... | collective-permute-start | bytes 393224 | tf_op jit(solution)/shard_map/ppermute | solution.py:429
  81.8 4.1 %collective-permute-done.15.refs_0_ = bf16[256,128]{1,0:T(8,128)(2,1)S(1)} collective-permute-done((bf16[256,128]{1,0:T(8,128)(2,1)S(1)}, bf16[256,128]{1,0:T(8,128)(2,1)S(1)}, u32[]{:S(2)}, u32[]{:S(2)}) %collective-permute-start.15) | collective-permute-done | bytes 65568 | tf_op jit(solution)/shard_map/ppermute | solution.py:433
  85.9 2.7 %finish.1 = (bf16[16,144,128]{2,1,0:T(8,128)(2,1)S(1)}, bf16[128,768]{1,0:T(8,128)(2,1)S(1)}) custom-call(s32[6]{0:T(128)S(1)} %stack.45.pos_ref, s32[4]{0:T(128)S(1)} %copy-done.9, bf16[256,4096]{1,0:T(8,128)(2,1)S(1)} %bitcast.20, bf16[512,4096]{1,0:T(8,128)(2,1)S(1)} %bitcast.17, f32[8,128]{1,0:T(8,128)S(1)} %get-tuple-element.50.loss_ref, ...), custom_call_target="tpu_custom_call" | custom-call | tf_op jit(solution)/shard_map/finish/pallas_call | solution.py:527
  88.6 2.9 %collective-permute-start.21 = (bf16[16,144,128]{2,1,0:T(8,128)(2,1)S(1)}, bf16[16,144,128]{2,1,0:T(8,128)(2,1)S(1)}, u32[]{:S(2)}, u32[]{:S(2)}) collective-permute-start(bf16[16,144,128]{2,1,0:T(8,128)(2,1)S(1)} %get-tuple-element.71), channel_id=1, source_target_pairs={{0,1},{1,0},{2,3},{3,2},{4,5},{5,4},{6,7},{7,6},{8,9},{9,8},{10,11... | collective-permute-start | bytes 1769480 | tf_op jit(solution)/shard_map/ppermute | solution.py:425
  91.5 1.7 %finish_more.1 = bf16[16,144,128]{2,1,0:T(8,128)(2,1)S(1)} custom-call(s32[6]{0:T(128)S(1)} %stack.45.pos_ref, bf16[256,4096]{1,0:T(8,128)(2,1)S(1)} %bitcast.21, bf16[512,4096]{1,0:T(8,128)(2,1)S(1)} %bitcast.18, f32[8,128]{1,0:T(8,128)S(1)} %get-tuple-element.50.loss_ref, bf16[128,768]{1,0:T(8,128)(2,1)S(1)} %get-tuple-element.70.backs_ref), custom_call_target="tpu_custom_call" | custom-call | tf_op jit(solution)/shard_map/finish_more/pallas_call | solution.py:532
  93.3 15.5 %all_to_all.21.x_ref = bf16[16,144,128]{2,1,0:T(8,128)(2,1)S(1)} all-to-all(bf16[16,144,128]{2,1,0:T(8,128)(2,1)S(1)} %add_convert_fusion), channel_id=1, replica_groups=mesh['yh'=2,'x'=4,'a'=4,'b'=2,'yl'=2,'c'=2] {'yh','x','yl'}, dimensions={0} | all-to-all | bytes 1179648 | tf_op jit(solution)/shard_map/all_to_all | solution.py:537
  109.0 12.1 %all_to_all.22.x_ref = bf16[8,144,128]{2,1,0:T(8,128)(2,1)S(1)} all-to-all(bf16[8,144,128]{2,1,0:T(8,128)(2,1)S(1)} %sum_rows.1), channel_id=1, replica_groups=mesh['yh'=2,'x'=4,'a'=4,'b'=2,'yl'=2,'c'=2] {'a','b'}, dimensions={0} | all-to-all | bytes 589824 | tf_op jit(solution)/shard_map/all_to_all | solution.py:539
  121.3 13.0 %all_to_all.23 = bf16[16,128,128]{2,1,0:T(8,128)(2,1)S(1)} all-to-all(bf16[16,128,128]{2,1,0:T(8,128)(2,1)S(1)} %get-tuple-element.72), channel_id=1, replica_groups=mesh['yh'=2,'x'=4,'a'=4,'b'=2,'yl'=2,'c'=2] {'yh','x','yl'}, dimensions={0} | all-to-all | bytes 1048576 | tf_op jit(solution)/shard_map/all_to_all | solution.py:544
  134.3 4.6 %collective-permute-start.22 = (bf16[16,128,128]{2,1,0:T(8,128)(2,1)S(1)}, bf16[16,128,128]{2,1,0:T(8,128)(2,1)S(1)}, u32[]{:S(2)}, u32[]{:S(2)}) collective-permute-start(bf16[16,128,128]{2,1,0:T(8,128)(2,1)S(1)} %all_to_all.23), channel_id=1, source_target_pairs={{0,1},{1,0},{2,3},{3,2},{4,5},{5,4},{6,7},{7,6},{8,9},{9,8},{10,11... | collective-permute-start | bytes 1572872 | tf_op jit(solution)/shard_map/ppermute | solution.py:425
  139.4 1.0 collective-permute-done.22
  140.6 1.5 %bitcast_convert_fusion = f32[4096,128]{1,0:T(8,128)} fusion(bf16[32,128,128]{2,1,0:T(8,128)(2,1)S(1)} %pad_maximum_fusion), kind=kLoop, calls=%fused_computation.2 | loop fusion | flops 524288 | bytes 3145728 | tf_op jit(solution)/shard_map/convert_element_type | solution.py:548
  (57 shorter events, 7.0 us)
Async XLA Ops:
  6.4 52.7 %copy-start.5 = (bf16[304,128]{1,0:T(8,128)(2,1)S(1)}, bf16[304,128]{1,0:T(8,128)(2,1)}, u32[]{:S(2)}) copy-start(bf16[304,128]{1,0:T(8,128)(2,1)} %get-tuple-element.39.refs_0_) | copy-start | bytes 233476
  6.4 52.7 %copy-start.8 = (f32[8,128]{1,0:T(8,128)S(1)}, f32[8,128]{1,0:T(8,128)}, u32[]{:S(2)}) copy-start(f32[8,128]{1,0:T(8,128)} %get-tuple-element.38.const_ref) | copy-start | bytes 12292
  6.4 8.0 %collective-permute-start = (bf16[304,128]{1,0:T(8,128)(2,1)}, bf16[304,128]{1,0:T(8,128)(2,1)S(1)}, u32[]{:S(2)}, u32[]{:S(2)}) collective-permute-start(bf16[304,128]{1,0:T(8,128)(2,1)} %get-tuple-element.39.refs_0_), channel_id=1, source_target_pairs={{0,8},{8,0},{16,24},{24,16},{1,9},{9,1},{17,25},{25,17},{2,10},{10... | collective-permute-start | bytes 233480 | tf_op jit(solution)/shard_map/ppermute | solution.py:433
  10.3 14.0 %collective-permute-start.5 = (bf16[304,128]{1,0:T(8,128)(2,1)}, bf16[304,128]{1,0:T(8,128)(2,1)S(1)}, u32[]{:S(2)}, u32[]{:S(2)}) collective-permute-start(bf16[304,128]{1,0:T(8,128)(2,1)} %get-tuple-element.42.refs_3_), channel_id=1, source_target_pairs={{0,32},{32,0},{64,96},{96,64},{1,33},{33,1},{65,97},{97,65},{2,34}... | collective-permute-start | bytes 233480 | tf_op jit(solution)/shard_map/ppermute | solution.py:433
  11.5 13.8 %collective-permute-start.11 = (bf16[528,128]{1,0:T(8,128)(2,1)}, bf16[528,128]{1,0:T(8,128)(2,1)S(1)}, u32[]{:S(2)}, u32[]{:S(2)}) collective-permute-start(bf16[528,128]{1,0:T(8,128)(2,1)} %get-tuple-element.40.refs_3_.refs_10_.refs_6_), channel_id=1, source_target_pairs={{0,128},{128,0},{1,129},{129,1},{2,130},{130,2},{3,131},{131,3},{4... | collective-permute-start | bytes 405512 | tf_op jit(solution)/shard_map/ppermute | solution.py:425
  15.3 20.4 %collective-permute-start.1 = (bf16[2,304,128]{2,1,0:T(8,128)(2,1)S(1)}, bf16[2,304,128]{2,1,0:T(8,128)(2,1)S(1)}, u32[]{:S(2)}, u32[]{:S(2)}) collective-permute-start(bf16[2,304,128]{2,1,0:T(8,128)(2,1)S(1)} %pad_maximum_fusion.1), channel_id=1, source_target_pairs={{0,16},{8,24},{16,0},{24,8},{1,17},{9,25},{17,1},{25,9},{2,18},{10... | collective-permute-start | bytes 466952 | tf_op jit(solution)/shard_map/ppermute | solution.py:433
  21.8 10.0 %collective-permute-start.4 = (bf16[528,128]{1,0:T(8,128)(2,1)}, bf16[528,128]{1,0:T(8,128)(2,1)S(1)}, u32[]{:S(2)}, u32[]{:S(2)}) collective-permute-start(bf16[528,128]{1,0:T(8,128)(2,1)} %get-tuple-element.40.refs_3_.refs_10_.refs_6_), channel_id=1, source_target_pairs={{0,6},{2,4},{4,2},{6,0},{1,7},{3,5},{5,3},{7,1},{8,14},{10,12},{12... | collective-permute-start | bytes 405512 | tf_op jit(solution)/shard_map/ppermute | solution.py:429
  21.8 12.5 %collective-permute-start.3 = (bf16[528,128]{1,0:T(8,128)(2,1)}, bf16[528,128]{1,0:T(8,128)(2,1)S(1)}, u32[]{:S(2)}, u32[]{:S(2)}) collective-permute-start(bf16[528,128]{1,0:T(8,128)(2,1)} %get-tuple-element.40.refs_3_.refs_10_.refs_6_), channel_id=1, source_target_pairs={{0,4},{4,0},{1,5},{5,1},{2,6},{6,2},{3,7},{7,3},{8,12},{12,8},{9,1... | collective-permute-start | bytes 405512 | tf_op jit(solution)/shard_map/ppermute | solution.py:425
  24.3 11.4 %collective-permute-start.2 = (bf16[528,128]{1,0:T(8,128)(2,1)}, bf16[528,128]{1,0:T(8,128)(2,1)S(1)}, u32[]{:S(2)}, u32[]{:S(2)}) collective-permute-start(bf16[528,128]{1,0:T(8,128)(2,1)} %get-tuple-element.40.refs_3_.refs_10_.refs_6_), channel_id=1, source_target_pairs={{0,2},{2,0},{1,3},{3,1},{4,6},{6,4},{5,7},{7,5},{8,10},{10,8},{9,1... | collective-permute-start | bytes 405512 | tf_op jit(solution)/shard_map/ppermute | solution.py:425
  25.4 15.0 %collective-permute-start.6 = (bf16[2,304,128]{2,1,0:T(8,128)(2,1)S(1)}, bf16[2,304,128]{2,1,0:T(8,128)(2,1)S(1)}, u32[]{:S(2)}, u32[]{:S(2)}) collective-permute-start(bf16[2,304,128]{2,1,0:T(8,128)(2,1)S(1)} %pad_maximum_fusion.2), channel_id=1, source_target_pairs={{0,64},{32,96},{64,0},{96,32},{1,65},{33,97},{65,1},{97,33},{2,66}... | collective-permute-start | bytes 466952 | tf_op jit(solution)/shard_map/ppermute | solution.py:433
  31.8 8.6 %collective-permute-start.7 = (bf16[528,128]{1,0:T(8,128)(2,1)}, bf16[528,128]{1,0:T(8,128)(2,1)S(1)}, u32[]{:S(2)}, u32[]{:S(2)}) collective-permute-start(bf16[528,128]{1,0:T(8,128)(2,1)} %get-tuple-element.40.refs_3_.refs_10_.refs_6_), channel_id=1, source_target_pairs={{0,1},{1,0},{2,3},{3,2},{4,5},{5,4},{6,7},{7,6},{8,9},{9,8},{10,11... | collective-permute-start | bytes 405512 | tf_op jit(solution)/shard_map/ppermute | solution.py:425
  34.3 6.1 %collective-permute-start.10 = (bf16[528,128]{1,0:T(8,128)(2,1)S(1)}, bf16[528,128]{1,0:T(8,128)(2,1)S(1)}, u32[]{:S(2)}, u32[]{:S(2)}) collective-permute-start(bf16[528,128]{1,0:T(8,128)(2,1)S(1)} %collective-permute-done.4.refs_6_.refs_9_), channel_id=1, source_target_pairs={{0,1},{1,0},{2,3},{3,2},{4,5},{5,4},{6,7},{7,6},{8,9},{9,8},{10,11... | collective-permute-start | bytes 405512 | tf_op jit(solution)/shard_map/ppermute | solution.py:425
  35.7 4.7 %collective-permute-start.9 = (bf16[528,128]{1,0:T(8,128)(2,1)S(1)}, bf16[528,128]{1,0:T(8,128)(2,1)S(1)}, u32[]{:S(2)}, u32[]{:S(2)}) collective-permute-start(bf16[528,128]{1,0:T(8,128)(2,1)S(1)} %collective-permute-done.3.refs_5_.refs_8_), channel_id=1, source_target_pairs={{0,1},{1,0},{2,3},{3,2},{4,5},{5,4},{6,7},{7,6},{8,9},{9,8},{10,11... | collective-permute-start | bytes 405512 | tf_op jit(solution)/shard_map/ppermute | solution.py:425
  35.7 4.7 %collective-permute-start.8 = (bf16[528,128]{1,0:T(8,128)(2,1)S(1)}, bf16[528,128]{1,0:T(8,128)(2,1)S(1)}, u32[]{:S(2)}, u32[]{:S(2)}) collective-permute-start(bf16[528,128]{1,0:T(8,128)(2,1)S(1)} %collective-permute-done.2.refs_4_.refs_7_), channel_id=1, source_target_pairs={{0,1},{1,0},{2,3},{3,2},{4,5},{5,4},{6,7},{7,6},{8,9},{9,8},{10,11... | collective-permute-start | bytes 405512 | tf_op jit(solution)/shard_map/ppermute | solution.py:425
  36.3 0.9 copy-start.2
  40.4 0.9 copy-start.6
  59.1 5.8 %copy-start.3 = (bf16[528,128]{1,0:T(8,128)(2,1)S(1)}, bf16[528,128]{1,0:T(8,128)(2,1)}, u32[]{:S(2)}) copy-start(bf16[528,128]{1,0:T(8,128)(2,1)} %get-tuple-element.40.refs_3_.refs_10_.refs_6_) | copy-start | bytes 405508
  63.2 8.9 %collective-permute-start.14 = (bf16[4,512,128]{2,1,0:T(8,128)(2,1)S(1)}, bf16[4,512,128]{2,1,0:T(8,128)(2,1)S(1)}, u32[]{:S(2)}, u32[]{:S(2)}) collective-permute-start(bf16[4,512,128]{2,1,0:T(8,128)(2,1)S(1)} %get-tuple-element.62), channel_id=1, source_target_pairs={{0,1},{1,0},{2,3},{3,2},{4,5},{5,4},{6,7},{7,6},{8,9},{9,8},{10,11... | collective-permute-start | bytes 1572872 | tf_op jit(solution)/shard_map/ppermute | solution.py:425
  64.9 21.0 %copy-start = (bf16[4,128,4096]{2,1,0:T(8,128)(2,1)S(1)}, bf16[4,128,4096]{2,1,0:T(8,128)(2,1)}, u32[]{:S(2)}) copy-start(bf16[4,128,4096]{2,1,0:T(8,128)(2,1)} %param.9) | copy-start | bytes 12582916
  64.9 21.0 %copy-start.7 = (f32[768,128]{1,0:T(8,128)S(1)}, f32[768,128]{1,0:T(8,128)}, u32[]{:S(2)}) copy-start(f32[768,128]{1,0:T(8,128)} %get-tuple-element.51.raw_ref) | copy-start | bytes 1179652
  67.7 18.2 %copy-start.1 = (bf16[8,32,4096]{2,1,0:T(8,128)(2,1)S(1)}, bf16[8,32,4096]{2,1,0:T(8,128)(2,1)}, u32[]{:S(2)}) copy-start(bf16[8,32,4096]{2,1,0:T(8,128)(2,1)} %param.8) | copy-start | bytes 6291460
  67.7 18.2 %copy-start.9 = (s32[4]{0:T(128)S(1)}, s32[4]{0:T(128)}, u32[]{:S(2)}) copy-start(s32[4]{0:T(128)} %p_len_ref.3) | copy-start | bytes 52
  67.7 9.4 %collective-permute-start.12 = (bf16[2,256,128]{2,1,0:T(8,128)(2,1)S(1)}, bf16[2,256,128]{2,1,0:T(8,128)(2,1)S(1)}, u32[]{:S(2)}, u32[]{:S(2)}) collective-permute-start(bf16[2,256,128]{2,1,0:T(8,128)(2,1)S(1)} %get-tuple-element.58), channel_id=1, source_target_pairs={{0,16},{8,24},{16,0},{24,8},{1,17},{9,25},{17,1},{25,9},{2,18},{10... | collective-permute-start | bytes 393224 | tf_op jit(solution)/shard_map/ppermute | solution.py:433
  68.3 13.1 %collective-permute-start.13 = (bf16[2,256,128]{2,1,0:T(8,128)(2,1)S(1)}, bf16[2,256,128]{2,1,0:T(8,128)(2,1)S(1)}, u32[]{:S(2)}, u32[]{:S(2)}) collective-permute-start(bf16[2,256,128]{2,1,0:T(8,128)(2,1)S(1)} %get-tuple-element.59), channel_id=1, source_target_pairs={{0,64},{32,96},{64,0},{96,32},{1,65},{33,97},{65,1},{97,33},{2,66}... | collective-permute-start | bytes 393224 | tf_op jit(solution)/shard_map/ppermute | solution.py:433
  69.3 12.3 %collective-permute-start.20 = (bf16[512,128]{1,0:T(8,128)(2,1)S(1)}, bf16[512,128]{1,0:T(8,128)(2,1)S(1)}, u32[]{:S(2)}, u32[]{:S(2)}) collective-permute-start(bf16[512,128]{1,0:T(8,128)(2,1)S(1)} %get-tuple-element.69), channel_id=1, source_target_pairs={{0,128},{128,0},{1,129},{129,1},{2,130},{130,2},{3,131},{131,3},{4... | collective-permute-start | bytes 393224 | tf_op jit(solution)/shard_map/ppermute | solution.py:425
  72.3 13.6 %collective-permute-start.17 = (bf16[512,128]{1,0:T(8,128)(2,1)S(1)}, bf16[512,128]{1,0:T(8,128)(2,1)S(1)}, u32[]{:S(2)}, u32[]{:S(2)}) collective-permute-start(bf16[512,128]{1,0:T(8,128)(2,1)S(1)} %get-tuple-element.66), channel_id=1, source_target_pairs={{0,2},{2,0},{1,3},{3,1},{4,6},{6,4},{5,7},{7,5},{8,10},{10,8},{9,1... | collective-permute-start | bytes 393224 | tf_op jit(solution)/shard_map/ppermute | solution.py:425
  72.8 13.1 %collective-permute-start.18 = (bf16[512,128]{1,0:T(8,128)(2,1)S(1)}, bf16[512,128]{1,0:T(8,128)(2,1)S(1)}, u32[]{:S(2)}, u32[]{:S(2)}) collective-permute-start(bf16[512,128]{1,0:T(8,128)(2,1)S(1)} %get-tuple-element.67), channel_id=1, source_target_pairs={{0,4},{4,0},{1,5},{5,1},{2,6},{6,2},{3,7},{7,3},{8,12},{12,8},{9,1... | collective-permute-start | bytes 393224 | tf_op jit(solution)/shard_map/ppermute | solution.py:425
  77.1 8.8 %collective-permute-start.19 = (bf16[512,128]{1,0:T(8,128)(2,1)S(1)}, bf16[512,128]{1,0:T(8,128)(2,1)S(1)}, u32[]{:S(2)}, u32[]{:S(2)}) collective-permute-start(bf16[512,128]{1,0:T(8,128)(2,1)S(1)} %get-tuple-element.68), channel_id=1, source_target_pairs={{0,6},{2,4},{4,2},{6,0},{1,7},{3,5},{5,3},{7,1},{8,14},{10,12},{12... | collective-permute-start | bytes 393224 | tf_op jit(solution)/shard_map/ppermute | solution.py:429
  81.5 4.4 %collective-permute-start.15 = (bf16[256,128]{1,0:T(8,128)(2,1)S(1)}, bf16[256,128]{1,0:T(8,128)(2,1)S(1)}, u32[]{:S(2)}, u32[]{:S(2)}) collective-permute-start(bf16[256,128]{1,0:T(8,128)(2,1)S(1)} %get-tuple-element.64), channel_id=1, source_target_pairs={{0,8},{8,0},{16,24},{24,16},{1,9},{9,1},{17,25},{25,17},{2,10},{10... | collective-permute-start | bytes 196616 | tf_op jit(solution)/shard_map/ppermute | solution.py:433
  81.6 4.3 %collective-permute-start.16 = (bf16[256,128]{1,0:T(8,128)(2,1)S(1)}, bf16[256,128]{1,0:T(8,128)(2,1)S(1)}, u32[]{:S(2)}, u32[]{:S(2)}) collective-permute-start(bf16[256,128]{1,0:T(8,128)(2,1)S(1)} %get-tuple-element.65), channel_id=1, source_target_pairs={{0,32},{32,0},{64,96},{96,64},{1,33},{33,1},{65,97},{97,65},{2,34}... | collective-permute-start | bytes 196616 | tf_op jit(solution)/shard_map/ppermute | solution.py:433
  88.6 4.6 %collective-permute-start.21 = (bf16[16,144,128]{2,1,0:T(8,128)(2,1)S(1)}, bf16[16,144,128]{2,1,0:T(8,128)(2,1)S(1)}, u32[]{:S(2)}, u32[]{:S(2)}) collective-permute-start(bf16[16,144,128]{2,1,0:T(8,128)(2,1)S(1)} %get-tuple-element.71), channel_id=1, source_target_pairs={{0,1},{1,0},{2,3},{3,2},{4,5},{5,4},{6,7},{7,6},{8,9},{9,8},{10,11... | collective-permute-start | bytes 1769480 | tf_op jit(solution)/shard_map/ppermute | solution.py:425
  134.3 6.1 %collective-permute-start.22 = (bf16[16,128,128]{2,1,0:T(8,128)(2,1)S(1)}, bf16[16,128,128]{2,1,0:T(8,128)(2,1)S(1)}, u32[]{:S(2)}, u32[]{:S(2)}) collective-permute-start(bf16[16,128,128]{2,1,0:T(8,128)(2,1)S(1)} %all_to_all.23), channel_id=1, source_target_pairs={{0,1},{1,0},{2,3},{3,2},{4,5},{5,4},{6,7},{7,6},{8,9},{9,8},{10,11... | collective-permute-start | bytes 1572872 | tf_op jit(solution)/shard_map/ppermute | solution.py:425
  (1 other events, 0.9 us)
where the time goes:
time: 142 us
  blocking collectives  54.5 us (38%)
  starting transfers between devices  43.3 us (30%)
  Pallas kernels  23.6 us (17%)
  waiting for transfers between devices  12.8 us (9%)
  other arithmetic  3.65 us (3%)
  local copies, waits for them, and re-layouts  3.3 us (2%)
    all_to_all x2, blocking collectives, local(): part = lax.all_to_all(part, ('yh', 'x', 'yl'), 0, 0, tiled=True)  28.5 us
    ppermute x13, starting transfers between devices, flip(): return lax.ppermute(x, axis, [(0, 1), (1, 0)])  22.8 us
    ppermute x8, starting transfers between devices, swap(): return lax.ppermute(x, axis, [(i, i ^ d) for i in range(4)])  16.2 us
    all_to_all x1, blocking collectives, local(): rows = lax.all_to_all(rows, ('x', 'a'), 0, 0, tiled=True)  13.9 us
    all_to_all x1, blocking collectives, local(): part = lax.all_to_all(part, ('a', 'b'), 0, 0, tiled=True)  12.1 us
    ppermute x8, waiting for transfers between devices, swap(): return lax.ppermute(x, axis, [(i, i ^ d) for i in range(4)])  7.87 us
    pallas_call x1, Pallas kernels, local(): pl.pallas_call(project, in_specs=[SMEM] * 3 + [ANY] * 5, out_specs=[VMEM]...  5.74 us
    ppermute x2, starting transfers between devices, flip2(): return lax.ppermute(x, ('b', 'yl'), [(i, i ^ 3) for i in range(4)])  4.31 us
  transfers between devices with their start and end apart: 23, of which 5 were waited for; matrix products, arithmetic and copies ran while one was open for 2% of the time, Pallas kernels for 5%

commit v1 on v0

--- a/solution.py
+++ b/solution.py
@@ -1,4 +1,3 @@
-import functools
 import math
 
 import jax
@@ -30,6 +29,9 @@
 LIMIT = 24
 COLS = 1024
 DEAD = -1e4
+HALF = E // 2
+PARTS, AROUND = 32, 4
+SCATTER = ("yh", "x", "b", "yl")
 
 
 def sds(shape, dtype):
@@ -86,11 +88,11 @@
     moves = [
         (teacher_hbm, teacher_ref),
         (ids_hbm, ids_ref),
-        (w_hbm, w_ref),
-        (x_p_hbm.at[:half], x_p_ref.at[:half]),
-        (x_p_hbm.at[half:], x_p_ref.at[half:]),
-        (x_q_hbm, x_q_ref),
     ]
+    for hbm, ref, rows in ((w_hbm, w_ref, D // 2), (x_p_hbm, x_p_ref, PT // 4), (x_q_hbm, x_q_ref, QT // 2)):
+        moves += [
+            (hbm.at[k : k + rows], ref.at[k : k + rows]) for k in range(0, hbm.shape[0], rows)
+        ]
     copies = [pltpu.make_async_copy(a, b, sems.at[k]) for k, (a, b) in enumerate(moves)]
     for copy in copies:
         copy.start()
@@ -130,14 +132,17 @@
         prob = prob + jnp.where(hit, far_prob[:, k : k + 1], 0.0)
     put_pieces(far_ref, prob, number)
     copies[2].wait()
+    copies[3].wait()
     w = w_ref[...]
     for k in range(2):
-        copies[3 + k].wait()
+        copies[4 + 2 * k].wait()
+        copies[5 + 2 * k].wait()
         at = slice(k * half, (k + 1) * half)
         raw = nn(x_p_ref[at, :], w)
         raw_ref[at, :] = raw
         p_ref[at, :] = jnp.where(live_rows(p_len_ref, 2 * k, half), unit_raw(raw), 0.0).astype(bf16)
-    copies[5].wait()
+    copies[8].wait()
+    copies[9].wait()
     raw = nn(x_q_ref[...], w)
     raw_ref[PT:, :] = raw
     vecs = unit_raw(raw).astype(bf16)
@@ -245,10 +250,10 @@
 def split(refs, *sizes):
     out, k = [], 0
     for n in sizes:
-        group = list(refs[k : k + (3 if n == "q" else n)])
+        group = list(refs[k : k + (2 if n == "q" else n)])
         k += len(group)
         if n == "q":
-            group = group[:2] + [group[2].at[0], group[2].at[1]]
+            group = [pair.at[i] for pair in group for i in range(2)]
         out.append(group)
     return out
 
@@ -282,8 +287,11 @@
 
 def backward_first(pos_ref, const_ref, rows_ref, scores_ref, more_ref, tot_ref, more_tot_ref, far_tot_ref,
                    info_ref, *refs):
-    near_q, far_q, p_refs, (w_ref,), outs = split(refs, "q", "q", PB // 2, 1, 8)
-    (p_send, q_part, coef_ref, far_coef_ref, loss_ref, more_coef_ref, g_ref, q_ref) = outs
+    near_q, far_q, p_refs, far_p, (w_ref, far_w_ref), outs = split(
+        refs, "q", "q", PB // 2, 2, 2, 12
+    )
+    (p_send, p_yh, far_send, far_keep, p_part, q_part, coef_ref, loss_ref,
+     more_coef_ref, far_coef_ref, g_ref, q_ref) = outs
     x, a = pos_ref[0], pos_ref[1]
     by_x = [sum(rows_ref[4 * i + j, 0:1, :LANES] for j in range(4)) for i in range(4)]
     by_a = [sum(rows_ref[4 * i + j, 1:2, :LANES] for i in range(4)) for j in range(4)]
@@ -311,32 +319,33 @@
     def put(pb, value):
         p_send[pb] = value.astype(bf16)
 
+    def far_put(pb, value):
+        if pb == 0:
+            p_part[...] = value
+        else:
+            p_yh[...] = value.astype(bf16)
+
     zero = jnp.zeros((E, QB * QT), f32)
     q_part[...] = block_grads(near_q, p_refs, w_ref, more_coef_ref, put, g_ref, q_ref, zero)
-
-
-def backward_second(coef_ref, far_coef_ref, q_part, *refs):
-    near_q, far_q, p_refs, far_p, (w_ref, far_w_ref), outs = split(refs, "q", "q", PB // 2, 2, 2, 7)
-    (q_keep, near_send, far_send, p_keep, p_yh, g_ref, q_ref) = outs
-
-    def near_put(pb, value):
-        p_keep[pb] = value
-
-    def far_put(pb, value):
-        if pb == 0:
-            p_keep[0] = p_keep[0] + value
-        else:
-            p_yh[...] = value.astype(bf16)
-
-    q_grad = block_grads(near_q, p_refs, w_ref, coef_ref, near_put, g_ref, q_ref, q_part[...]).T
-    zero = jnp.zeros((E, QB * QT), f32)
-    far_q_grad = block_grads(far_q, far_p, far_w_ref, far_coef_ref, far_put, g_ref, q_ref, zero).T
-    q_keep[0] = q_grad[:QT] + far_q_grad[:QT]
-    q_keep[1] = q_grad[QT : 2 * QT]
-    q_keep[2] = far_q_grad[QT : 2 * QT]
+    q_grad = block_grads(far_q, far_p, far_w_ref, far_coef_ref, far_put, g_ref, q_ref, zero).T
+    put_queries(q_grad, far_keep, far_send)
+
+
+def put_queries(q_grad, keep_ref, send_ref):
     for k in range(2):
-        near_send[k] = q_grad[(2 + k) * QT : (3 + k) * QT].astype(bf16)
-        far_send[k] = far_q_grad[(2 + k) * QT : (3 + k) * QT].astype(bf16)
+        keep_ref[k] = q_grad[k * QT : (k + 1) * QT]
+        send_ref[k] = q_grad[(2 + k) * QT : (3 + k) * QT].astype(bf16)
+
+
+def backward_second(coef_ref, q_part, p_part, *refs):
+    near_q, p_refs, (w_ref,), outs = split(refs, "q", PB // 2, 1, 5)
+    (near_keep, near_send, p_keep, g_ref, q_ref) = outs
+
+    def put(pb, value):
+        p_keep[pb] = value + p_part[...] if pb == 0 else value
+
+    q_grad = block_grads(near_q, p_refs, w_ref, coef_ref, put, g_ref, q_ref, q_part[...]).T
+    put_queries(q_grad, near_keep, near_send)
 
 
 def merge_passages(keep_ref, more_ref, *outs):
@@ -344,20 +353,19 @@
         outs[k][...] = (keep_ref[k] + more_ref[k].astype(f32)).astype(outs[k].dtype)
 
 
-def merge_queries(keep_ref, near_ref, far_ref, own_ref, near_out, far_out):
-    own_ref[...] = keep_ref[0] + near_ref[0].astype(f32) + far_ref[0].astype(f32)
-    near_out[...] = (keep_ref[1] + near_ref[1].astype(f32)).astype(bf16)
-    far_out[...] = (keep_ref[2] + far_ref[1].astype(f32)).astype(bf16)
-
-
-def finish(pos_ref, p_len_ref, x_q_ref, x_p_ref, loss_ref, raw_ref, q_own, p_own, *refs):
-    q_in, p_in = refs[:2], refs[2:6]
-    out_ref, backs_ref = refs[6:]
+def merge_queries(keep_ref, more_ref, own_ref, out_ref):
+    own_ref[...] = keep_ref[0] + more_ref[0].astype(f32)
+    out_ref[...] = (keep_ref[1] + more_ref[1].astype(f32)).astype(bf16)
+
+
+def finish(pos_ref, p_len_ref, x_q_ref, x_p_ref, loss_ref, raw_ref, p_own, *refs):
+    q_in, p_in = refs[:4], refs[4:8]
+    out_ref, backs_ref = refs[8:]
     i = pl.program_id(0)
 
     @pl.when(i == 0)
     def _():
-        q_grad = q_own[...] + sum(r[...].astype(f32) for r in q_in)
+        q_grad = sum(r[...].astype(f32) for r in q_in)
         p_grad = p_own[...] + sum(r[...].astype(f32) for r in p_in)
         p_grad = jnp.where(live_rows(p_len_ref, 0, PT), p_grad, 0.0)
         backs_ref[:, :QT] = back(raw_ref[PT:, :], q_grad).T.astype(bf16)
@@ -380,33 +388,41 @@
     rows = jnp.where(at == lane + 1, mid, rows)
     rows = jnp.where(at == lane + 2, low, rows)
     for k in range(COLS // 128):
-        out_ref[k, :128, :] = grad[:, k * 128 : (k + 1) * 128].astype(bf16)
-        out_ref[k, 128:, :] = rows.astype(bf16)
-
-
-def sum_rows(n, x_ref, out_ref):
+        for half in range(2):
+            part = grad[half * HALF : (half + 1) * HALF, k * 128 : (k + 1) * 128]
+            out_ref[2 * k + half, :HALF, :] = part.astype(bf16)
+            out_ref[2 * k + half, HALF:, :] = rows.astype(bf16)
+
+
+def sum_parts(x_ref):
     total = x_ref[0].astype(f32)
-    for k in range(1, n):
+    for k in range(1, x_ref.shape[0]):
         total = total + x_ref[k].astype(f32)
-    body = total[:128].astype(bf16)
-    loss = jnp.sum(total[128:129, :], axis=1, keepdims=True)
+    return total[:HALF].astype(bf16), jnp.sum(total[HALF : HALF + 1, :], axis=1, keepdims=True)
+
+
+def sum_rows(x_ref, out_ref):
+    body, loss = sum_parts(x_ref)
     hi, mid, low = (v.astype(f32) for v in pieces(jnp.broadcast_to(loss, (16, E))))
     at = iota((16, E), 1)
     rows = jnp.where(at == 0, hi, jnp.where(at == 1, mid, jnp.where(at == 2, low, 0.0))).astype(bf16)
+    for k in range(AROUND):
+        out_ref[k, :HALF, :] = body
+        out_ref[k, HALF:, :] = rows
+
+
+def sum_last(x_ref, out_ref, loss_ref):
+    body, loss = sum_parts(x_ref)
+    for k in range(PARTS):
+        out_ref[k] = body
+    loss_ref[...] = jnp.broadcast_to(loss, (8, E)) / QUERIES
+
+
+def unfold(pos_ref, x_ref, *refs):
+    out_ref = refs[-1]
     for k in range(8):
-        out_ref[k, :128, :] = body
-        out_ref[k, 128:, :] = rows
-
-
-def sum_last(n, x_ref, out_ref, loss_ref):
-    total = x_ref[0].astype(f32)
-    for k in range(1, n):
-        total = total + x_ref[k].astype(f32)
-    body = total[:128].T.astype(bf16)
-    for k in range(16):
-        out_ref[k] = body
-    loss = jnp.sum(total[128:129, :], axis=1, keepdims=True)
-    loss_ref[...] = jnp.broadcast_to(loss, (8, E)) / QUERIES
+        block = jnp.concatenate([x_ref[2 * k], x_ref[2 * k + 1]], axis=0).astype(f32)
+        out_ref[k * 128 : (k + 1) * 128, :] = block.T
 
 
 def call(kernel, out_shape, n_in, smem=(0,), scratch=(), name=None):
@@ -434,8 +450,8 @@
 
 
 def doubled(x, axis):
-    other = swap(x, axis, 1)
-    return [x, other, swap(jnp.stack([x, other]), axis, 2)]
+    pair = jnp.stack([x, swap(x, axis, 1)])
+    return [pair, swap(pair, axis, 2)]
 
 
 def local(x_q, x_p, w, query_len, passage_len, neg_ids, neg_count, teacher):
@@ -451,7 +467,7 @@
                    sds((QROWS, E), bf16), sds((8, E), f32)],
         scratch_shapes=[
             pltpu.VMEM((QT, D), bf16), pltpu.VMEM((PT, D), bf16), pltpu.VMEM((D, E), bf16),
-            pltpu.VMEM((QD, CANDS), f32), pltpu.VMEM((QD, NEG), i32), pltpu.SemaphoreType.DMA((6,)),
+            pltpu.VMEM((QD, CANDS), f32), pltpu.VMEM((QD, NEG), i32), pltpu.SemaphoreType.DMA((10,)),
         ],
         compiler_params=pltpu.CompilerParams(vmem_limit_bytes=60 * MIB),
         name="project",
@@ -467,40 +483,43 @@
     w_near, tot, scores = call(
         forward_first,
         [sds((4, PT, tokens), f32), sds((half, tokens), f32), sds((half, LANES), f32)],
-        8, scratch=wide, name="forward_first",
+        7, scratch=wide, name="forward_first",
     )(pos, *near_q, *near_ps)
     w_more, more_tot, more, w_far, far_tot, info, rows = call(
         forward_second,
         [sds((4, PT, tokens), f32), sds((half, tokens), f32), sds((half, LANES), f32),
          sds((2, PT, tokens), f32), sds((2 * PD, tokens), f32), sds((3, 2 * PD, LANES), f32),
          sds((16, 8, E), f32)],
-        14, scratch=wide, name="forward_second",
+        12, scratch=wide, name="forward_second",
     )(pos, scores, *near_q, *far_q, *more_ps, *far_ps)
     rows = lax.all_to_all(rows, ("x", "a"), 0, 0, tiled=True)
     room = [pltpu.VMEM((PT, tokens), bf16), pltpu.VMEM((tokens, E), bf16)]
-    p_send, q_part, coef, far_coef, loss = call(
+    p_send, p_yh, far_send, far_keep, p_part, q_part, coef, loss = call(
         backward_first,
-        [sds((4, PT, E), bf16), sds((E, tokens), f32), sds((half, tokens), f32),
-         sds((2 * PD, tokens), f32), sds((8, E), f32)],
-        20, scratch=[pltpu.VMEM((half, tokens), f32)] + room, name="backward_first",
-    )(pos, const, rows, scores, more, tot, more_tot, far_tot, info, *near_q, *far_q, *more_ps, w_more)
-    p_more = flip(p_send, "c")
-    q_keep, near_send, far_send, p_keep, p_yh = call(
+        [sds((4, PT, E), bf16), sds((PT, E), bf16), sds((2, QT, E), bf16), sds((2, QT, E), f32),
+         sds((PT, E), f32), sds((E, tokens), f32), sds((half, tokens), f32), sds((8, E), f32)],
+        21, scratch=[pltpu.VMEM((half, tokens), f32), pltpu.VMEM((2 * PD, tokens), f32)] + room,
+        name="backward_first",
+    )(pos, const, rows, scores, more, tot, more_tot, far_tot, info, *near_q, *far_q, *more_ps, *far_ps,
+      w_more, w_far)
+    p_more, far_in, p_yh = flip(p_send, "c"), swap(far_send, "x", 2), flip(p_yh, "yh")
+    near_keep, near_send, p_keep = call(
         backward_second,
-        [sds((3, QT, E), f32), sds((2, QT, E), bf16), sds((2, QT, E), bf16), sds((4, PT, E), f32),
-         sds((PT, E), bf16)],
-        17, smem=(), scratch=room, name="backward_second",
-    )(coef, far_coef, q_part, *near_q, *far_q, *near_ps, *far_ps, w_near, w_far)
-
-    near_in, far_in = swap(near_send, "a", 2), swap(far_send, "x", 2)
+        [sds((2, QT, E), f32), sds((2, QT, E), bf16), sds((4, PT, E), f32)],
+        10, smem=(), scratch=room, name="backward_second",
+    )(coef, q_part, p_part, *near_q, *near_ps, w_near)
+
+    near_in = swap(near_send, "a", 2)
     p_own, p1, p2, p3 = call(
         merge_passages, [sds((PT, E), f32)] + [sds((PT, E), bf16)] * 3, 2, smem=(), name="merge_passages"
     )(p_keep, p_more)
-    p_in = [flip(p1, "yl"), flip(p2, "b"), flip2(p3), flip(p_yh, "yh")]
-    q_own, near_send, far_send = call(
-        merge_queries, [sds((QT, E), f32)] + [sds((QT, E), bf16)] * 2, 3, smem=(), name="merge_queries"
-    )(q_keep, near_in, far_in)
-    q_in = [swap(near_send, "a", 1), swap(far_send, "x", 1)]
+    p_in = [flip(p1, "yl"), flip(p2, "b"), flip2(p3), p_yh]
+    q_in = []
+    for keep, more, axis in ((far_keep, far_in, "x"), (near_keep, near_in, "a")):
+        own, out = call(
+            merge_queries, [sds((QT, E), f32), sds((QT, E), bf16)], 2, smem=(), name="merge_" + axis
+        )(keep, more)
+        q_in += [own, swap(out, axis, 1)]
 
     def whole(shape):
         return pl.BlockSpec(shape, lambda i, pos: (0,) * len(shape))
@@ -515,15 +534,15 @@
                 num_scalar_prefetch=1,
                 grid=(D // 2 // COLS,),
                 in_specs=extra + [columns(QT, half), columns(PT, half)] + [whole(s) for s in ins],
-                out_specs=[pl.BlockSpec((COLS // 128, 144, E), lambda i, pos: (i, 0, 0))]
+                out_specs=[pl.BlockSpec((COLS // HALF, HALF + 16, E), lambda i, pos: (i, 0, 0))]
                 + [whole(s) for s in outs],
             ),
-            out_shape=[sds((16, 144, E), bf16)] + out_shape,
+            out_shape=[sds((PARTS, HALF + 16, E), bf16)] + out_shape,
             compiler_params=pltpu.CompilerParams(vmem_limit_bytes=LIMIT * MIB),
             name=name,
         )
 
-    operands = [loss, raw, q_own, p_own, *q_in, *p_in]
+    operands = [loss, raw, p_own, *q_in, *p_in]
     send, backs = halves(
         finish, lambda pos: 1 - pos[4], [SMEM], [v.shape for v in operands], [(E, QT + PT)],
         [sds((E, QT + PT), bf16)], "finish",
@@ -534,18 +553,32 @@
     )(pos, x_q, x_p, loss, backs)
 
     part = (mine.astype(f32) + other.astype(f32)).astype(bf16)
-    part = lax.all_to_all(part, ("yh", "x", "yl"), 0, 0, tiled=True)
-    part = call(functools.partial(sum_rows, 16), sds((8, 144, E), bf16), 1, smem=(), name="sum_rows")(part)
-    part = lax.all_to_all(part, ("a", "b"), 0, 0, tiled=True)
+    part = lax.all_to_all(part, SCATTER, 0, 0, tiled=True)
+    part = call(sum_rows, sds((AROUND, HALF + 16, E), bf16), 1, smem=(), name="sum_rows")(part)
+    part = lax.all_to_all(part, "a", 0, 0, tiled=True)
     part, total = call(
-        functools.partial(sum_last, 8), [sds((16, 128, E), bf16), sds((8, E), f32)], 1, smem=(),
-        name="sum_last",
+        sum_last, [sds((PARTS, HALF, E), bf16), sds((8, E), f32)], 1, smem=(), name="sum_last"
     )(part)
-    part = lax.all_to_all(part, ("yh", "x", "yl"), 0, 0, tiled=True)
+    part = lax.all_to_all(part, SCATTER, 0, 0, tiled=True)
     other = flip(part, "c")
-    first = jnp.where(c == 0, part, other)
-    second = jnp.where(c == 0, other, part)
-    grad = jnp.concatenate([first, second]).astype(f32).reshape(D, E)
+
+    def unfolded(x, half, *whole):
+        return pl.pallas_call(
+            unfold,
+            grid_spec=pltpu.PrefetchScalarGridSpec(
+                num_scalar_prefetch=1,
+                grid=(2,),
+                in_specs=[pl.BlockSpec((16, HALF, E), lambda i, pos: (i, 0, 0))] + [ANY] * len(whole),
+                out_specs=pl.BlockSpec((D // 4, E), lambda i, pos: (half(pos) * 2 + i, 0)),
+            ),
+            out_shape=sds((D, E), f32),
+            input_output_aliases={2: 0} if whole else {},
+            compiler_params=pltpu.CompilerParams(vmem_limit_bytes=LIMIT * MIB),
+            name="unfold",
+        )(pos, x, *whole)
+
+    grad = unfolded(part, lambda pos: pos[4])
+    grad = unfolded(other, lambda pos: 1 - pos[4], grad)
     return grad, total[0, 0]
 
 

time: 142 us -> 140 us (0.986)
  Pallas kernels: 23.6 us -> 26.8 us
  local copies, waits for them, and re-layouts: 3.3 us -> 1.53 us
  other arithmetic: 3.65 us -> 2.01 us
    pallas_call x5 -> x8, Pallas kernels: 7.31 us -> 10.5 us  [the longest x1 4.95 us: local(): call(backward_first, [sds((4, PT, E), bf16), sds((PT, E), bf16), sds((2,...]
    unnamed x20 -> x12, local copies, waits for them, and re-layouts: 2.7 us -> 0.93 us
    convert_element_type x1 -> x0, other arithmetic: 1.52 us -> none  [local(): grad = jnp.concatenate([first, second]).astype(f32).reshape(D, E)]
where the time goes in v1:
time: 140 us
  blocking collectives  53.6 us (38%)
  starting transfers between devices  43.3 us (31%)
  Pallas kernels  26.8 us (19%)
  waiting for transfers between devices  11.8 us (8%)
  other arithmetic  2.01 us (1%)
  local copies, waits for them, and re-layouts  1.53 us (1%)
    all_to_all x2, blocking collectives, local(): part = lax.all_to_all(part, SCATTER, 0, 0, tiled=True)  29.8 us
    ppermute x13, starting transfers between devices, flip(): return lax.ppermute(x, axis, [(0, 1), (1, 0)])  22.7 us
    ppermute x8, starting transfers between devices, swap(): return lax.ppermute(x, axis, [(i, i ^ d) for i in range(4)])  16.2 us
    all_to_all x1, blocking collectives, local(): rows = lax.all_to_all(rows, ('x', 'a'), 0, 0, tiled=True)  13.7 us
    all_to_all x1, blocking collectives, local(): part = lax.all_to_all(part, 'a', 0, 0, tiled=True)  10.1 us
    ppermute x8, waiting for transfers between devices, swap(): return lax.ppermute(x, axis, [(i, i ^ d) for i in range(4)])  7.84 us
    pallas_call x1, Pallas kernels, local(): pl.pallas_call(project, in_specs=[SMEM] * 3 + [ANY] * 5, out_specs=[VMEM]...  5.72 us
    pallas_call x1, Pallas kernels, local(): call(backward_first, [sds((4, PT, E), bf16), sds((PT, E), bf16), sds((2,...  4.95 us
  transfers between devices with their start and end apart: 23, of which 5 were waited for; matrix products, arithmetic and copies ran while one was open for 2% of the time, Pallas kernels for 5%

profile of v1, /device:TPU:1, one launch (start us, length us, event | category | flops | bytes accessed | tf_op | source)
XLA Modules:
  0.0 139.9 jit_solution(11376414426230524978)
XLA Ops:
  0.6 5.7 %project.1 = (f32[768,128]{1,0:T(8,128)}, bf16[528,128]{1,0:T(8,128)(2,1)}, bf16[304,128]{1,0:T(8,128)(2,1)}, bf16[304,128]{1,0:T(8,128)(2,1)}, f32[8,128]{1,0:T(8,128)}) custom-call(s32[8]{0:T(128)} %q_len_ref.1, s32[4]{0:T(128)} %p_len_ref.3, s32[8]{0:T(128)} %count_ref.1, bf16[256,4096]{1,0:T(8,128)(2,1)} %bitcast.16, bf16[512,4096]{1,0:T(8,128)(2,1)} %bitcast.13, ...), custom_call_target="tpu_custom_call" | custom-call | tf_op jit(solution)/shard_map/project/pallas_call | solution.py:462
  6.4 3.9 %collective-permute-start = (bf16[304,128]{1,0:T(8,128)(2,1)}, bf16[304,128]{1,0:T(8,128)(2,1)S(1)}, u32[]{:S(2)}, u32[]{:S(2)}) collective-permute-start(bf16[304,128]{1,0:T(8,128)(2,1)} %get-tuple-element.41), channel_id=1, source_target_pairs={{0,8},{8,0},{16,24},{24,16},{1,9},{9,1},{17,25},{25,17},{2,10},{10... | collective-permute-start | bytes 233480 | tf_op jit(solution)/shard_map/ppermute | solution.py:449
  10.3 1.2 collective-permute-start.5
  11.5 2.9 %collective-permute-start.11 = (bf16[528,128]{1,0:T(8,128)(2,1)}, bf16[528,128]{1,0:T(8,128)(2,1)S(1)}, u32[]{:S(2)}, u32[]{:S(2)}) collective-permute-start(bf16[528,128]{1,0:T(8,128)(2,1)} %get-tuple-element.42.refs_2_.refs_8_), channel_id=1, source_target_pairs={{0,128},{128,0},{1,129},{129,1},{2,130},{130,2},{3,131},{131,3},{4... | collective-permute-start | bytes 405512 | tf_op jit(solution)/shard_map/ppermute | solution.py:441
  14.4 0.9 pad_maximum_fusion.refs_0_
  15.3 6.4 %collective-permute-start.1 = (bf16[2,304,128]{2,1,0:T(8,128)(2,1)S(1)}, bf16[2,304,128]{2,1,0:T(8,128)(2,1)S(1)}, u32[]{:S(2)}, u32[]{:S(2)}) collective-permute-start(bf16[2,304,128]{2,1,0:T(8,128)(2,1)S(1)} %pad_maximum_fusion.refs_0_), channel_id=1, source_target_pairs={{0,16},{8,24},{16,0},{24,8},{1,17},{9,25},{17,1},{25,9},{2,18},{10... | collective-permute-start | bytes 466952 | tf_op jit(solution)/shard_map/ppermute | solution.py:449
  21.8 2.5 %collective-permute-start.3 = (bf16[528,128]{1,0:T(8,128)(2,1)}, bf16[528,128]{1,0:T(8,128)(2,1)S(1)}, u32[]{:S(2)}, u32[]{:S(2)}) collective-permute-start(bf16[528,128]{1,0:T(8,128)(2,1)} %get-tuple-element.42.refs_2_.refs_8_), channel_id=1, source_target_pairs={{0,4},{4,0},{1,5},{5,1},{2,6},{6,2},{3,7},{7,3},{8,12},{12,8},{9,1... | collective-permute-start | bytes 405512 | tf_op jit(solution)/shard_map/ppermute | solution.py:441
  25.3 2.8 %collective-permute-start.6 = (bf16[2,304,128]{2,1,0:T(8,128)(2,1)S(1)}, bf16[2,304,128]{2,1,0:T(8,128)(2,1)S(1)}, u32[]{:S(2)}, u32[]{:S(2)}) collective-permute-start(bf16[2,304,128]{2,1,0:T(8,128)(2,1)S(1)} %pad_maximum_fusion.1.refs_2_), channel_id=1, source_target_pairs={{0,64},{32,96},{64,0},{96,32},{1,65},{33,97},{65,1},{97,33},{2,66}... | collective-permute-start | bytes 466952 | tf_op jit(solution)/shard_map/ppermute | solution.py:449
  28.2 3.6 %collective-permute-done.4.refs_5_ = bf16[528,128]{1,0:T(8,128)(2,1)S(1)} collective-permute-done((bf16[528,128]{1,0:T(8,128)(2,1)}, bf16[528,128]{1,0:T(8,128)(2,1)S(1)}, u32[]{:S(2)}, u32[]{:S(2)}) %collective-permute-start.4) | collective-permute-done | bytes 135200 | tf_op jit(solution)/shard_map/ppermute | solution.py:445
  31.8 2.3 %collective-permute-start.7 = (bf16[528,128]{1,0:T(8,128)(2,1)}, bf16[528,128]{1,0:T(8,128)(2,1)S(1)}, u32[]{:S(2)}, u32[]{:S(2)}) collective-permute-start(bf16[528,128]{1,0:T(8,128)(2,1)} %get-tuple-element.42.refs_2_.refs_8_), channel_id=1, source_target_pairs={{0,1},{1,0},{2,3},{3,2},{4,5},{5,4},{6,7},{7,6},{8,9},{9,8},{10,11... | collective-permute-start | bytes 405512 | tf_op jit(solution)/shard_map/ppermute | solution.py:441
  34.3 1.3 collective-permute-start.10
  36.3 0.9 copy-done.2
  37.2 2.3 %forward_first.1 = (f32[4,512,1024]{2,1,0:T(8,128)S(1)}, f32[16,1024]{1,0:T(8,128)S(1)}, f32[16,32]{1,0:T(8,128)S(1)}) custom-call(s32[6]{0:T(128)S(1)} %stack.45.pos_ref, bf16[2,304,128]{2,1,0:T(8,128)(2,1)S(1)} %pad_maximum_fusion.refs_0_, bf16[2,304,128]{2,1,0:T(8,128)(2,1)S(1)} %collective-permute-done.1.refs_1_, bf16[528,128]{1,0:T(8,128)(2,1)S(1)} %copy-done.2, ...), custom_call_target="tpu_custom_call" | custom-call | tf_op jit(solution)/shard_map/forward_first/pallas_call | solution.py:483
  39.5 3.9 %forward_second.1 = (f32[4,512,1024]{2,1,0:T(8,128)S(1)}, f32[16,1024]{1,0:T(8,128)S(1)}, f32[16,32]{1,0:T(8,128)S(1)}, f32[2,512,1024]{2,1,0:T(8,128)S(1)}, f32...) custom-call(s32[6]{0:T(128)S(1)} %stack.45.pos_ref, ...), custom_call_target="tpu_custom_call" | custom-call | tf_op jit(solution)/shard_map/forward_second/pallas_call | solution.py:488
  43.4 13.7 %all_to_all.20.rows_ref = f32[16,8,128]{2,1,0:T(8,128)S(1)} all-to-all(f32[16,8,128]{2,1,0:T(8,128)S(1)} %get-tuple-element.45), channel_id=1, replica_groups=mesh['yh'=2,'x'=4,'a'=4,'b'=2,'yl'=2,'c'=2] {'x','a'}, dimensions={0} | all-to-all | bytes 131072 | tf_op jit(solution)/shard_map/all_to_all | solution.py:495
  57.1 5.0 %backward_first.1 = (bf16[4,512,128]{2,1,0:T(8,128)(2,1)S(1)}, bf16[512,128]{1,0:T(8,128)(2,1)S(1)}, bf16[2,256,128]{2,1,0:T(8,128)(2,1)S(1)}, f32[2,256,128]{2,...) custom-call(s32[6]{0:T(128)S(1)} %stack.45.pos_ref, ...), custom_call_target="tpu_custom_call" | custom-call | tf_op jit(solution)/shard_map/backward_first/pallas_call | solution.py:497
  62.1 1.8 %collective-permute-start.12 = (bf16[4,512,128]{2,1,0:T(8,128)(2,1)S(1)}, bf16[4,512,128]{2,1,0:T(8,128)(2,1)S(1)}, u32[]{:S(2)}, u32[]{:S(2)}) collective-permute-start(bf16[4,512,128]{2,1,0:T(8,128)(2,1)S(1)} %get-tuple-element.60), channel_id=1, source_target_pairs={{0,1},{1,0},{2,3},{3,2},{4,5},{5,4},{6,7},{7,6},{8,9},{9,8},{10,11... | collective-permute-start | bytes 1572872 | tf_op jit(solution)/shard_map/ppermute | solution.py:441
  63.9 1.9 %backward_second.1 = (f32[2,256,128]{2,1,0:T(8,128)S(1)}, bf16[2,256,128]{2,1,0:T(8,128)(2,1)S(1)}, f32[4,512,128]{2,1,0:T(8,128)S(1)}) custom-call(f32[16,1024]{1,0:T(8,128)S(1)} %get-tuple-element.55.coef_ref, f32[128,1024]{1,0:T(8,128)S(1)} %get-tuple-element.56.q_part, f32[512,128]{1,0:T(8,128)S(1)} %get-tuple-element.57.p_part, ...), custom_call_target="tpu_custom_call" | custom-call | tf_op jit(solution)/shard_map/backward_second/pallas_call | solution.py:506
  66.4 0.9 collective-permute-start.13
  67.4 2.9 %collective-permute-start.20 = (bf16[512,128]{1,0:T(8,128)(2,1)S(1)}, bf16[512,128]{1,0:T(8,128)(2,1)S(1)}, u32[]{:S(2)}, u32[]{:S(2)}) collective-permute-start(bf16[512,128]{1,0:T(8,128)(2,1)S(1)} %get-tuple-element.73), channel_id=1, source_target_pairs={{0,128},{128,0},{1,129},{129,1},{2,130},{130,2},{3,131},{131,3},{4... | collective-permute-start | bytes 393224 | tf_op jit(solution)/shard_map/ppermute | solution.py:441
  71.5 3.7 %collective-permute-done.15.more_ref = bf16[2,256,128]{2,1,0:T(8,128)(2,1)S(1)} collective-permute-done((bf16[2,256,128]{2,1,0:T(8,128)(2,1)S(1)}, bf16[2,256,128]{2,1,0:T(8,128)(2,1)S(1)}, u32[]{:S(2)}, u32[]{:S(2)}) %collective-permute-start.15) | collective-permute-done | bytes 131104 | tf_op jit(solution)/shard_map/ppermute | solution.py:449
  75.2 4.3 %collective-permute-start.19 = (bf16[512,128]{1,0:T(8,128)(2,1)S(1)}, bf16[512,128]{1,0:T(8,128)(2,1)S(1)}, u32[]{:S(2)}, u32[]{:S(2)}) collective-permute-start(bf16[512,128]{1,0:T(8,128)(2,1)S(1)} %get-tuple-element.72), channel_id=1, source_target_pairs={{0,6},{2,4},{4,2},{6,0},{1,7},{3,5},{5,3},{7,1},{8,14},{10,12},{12... | collective-permute-start | bytes 393224 | tf_op jit(solution)/shard_map/ppermute | solution.py:445
  79.9 4.1 %collective-permute-done.16.refs_3_ = bf16[256,128]{1,0:T(8,128)(2,1)S(1)} collective-permute-done((bf16[256,128]{1,0:T(8,128)(2,1)S(1)}, bf16[256,128]{1,0:T(8,128)(2,1)S(1)}, u32[]{:S(2)}, u32[]{:S(2)}) %collective-permute-start.16) | collective-permute-done | bytes 65568 | tf_op jit(solution)/shard_map/ppermute | solution.py:449
  84.1 2.7 %finish.1 = (bf16[32,80,128]{2,1,0:T(8,128)(2,1)S(1)}, bf16[128,768]{1,0:T(8,128)(2,1)S(1)}) custom-call(s32[6]{0:T(128)S(1)} %stack.45.pos_ref, s32[4]{0:T(128)S(1)} %copy-done.5, bf16[256,4096]{1,0:T(8,128)(2,1)S(1)} %bitcast.17, bf16[512,4096]{1,0:T(8,128)(2,1)S(1)} %bitcast.14, f32[8,128]{1,0:T(8,128)S(1)} %get-tuple-element.53.loss_ref, ...), custom_call_target="tpu_custom_call" | custom-call | tf_op jit(solution)/shard_map/finish/pallas_call | solution.py:546
  86.7 2.8 %collective-permute-start.21 = (bf16[32,80,128]{2,1,0:T(8,128)(2,1)S(1)}, bf16[32,80,128]{2,1,0:T(8,128)(2,1)S(1)}, u32[]{:S(2)}, u32[]{:S(2)}) collective-permute-start(bf16[32,80,128]{2,1,0:T(8,128)(2,1)S(1)} %get-tuple-element.75), channel_id=1, source_target_pairs={{0,1},{1,0},{2,3},{3,2},{4,5},{5,4},{6,7},{7,6},{8,9},{9,8},{10,11... | collective-permute-start | bytes 1966088 | tf_op jit(solution)/shard_map/ppermute | solution.py:441
  89.5 1.6 %finish_more.1 = bf16[32,80,128]{2,1,0:T(8,128)(2,1)S(1)} custom-call(s32[6]{0:T(128)S(1)} %stack.45.pos_ref, bf16[256,4096]{1,0:T(8,128)(2,1)S(1)} %bitcast.18, bf16[512,4096]{1,0:T(8,128)(2,1)S(1)} %bitcast.15, f32[8,128]{1,0:T(8,128)S(1)} %get-tuple-element.53.loss_ref, bf16[128,768]{1,0:T(8,128)(2,1)S(1)} %get-tuple-element.74.backs_ref), custom_call_target="tpu_custom_call" | custom-call | tf_op jit(solution)/shard_map/finish_more/pallas_call | solution.py:551
  91.4 16.5 %all_to_all.21.x_ref = bf16[32,80,128]{2,1,0:T(8,128)(2,1)S(1)} all-to-all(bf16[32,80,128]{2,1,0:T(8,128)(2,1)S(1)} %add_convert_fusion), channel_id=1, replica_groups=mesh['yh'=2,'x'=4,'a'=4,'b'=2,'yl'=2,'c'=2] {'yh','x','b','yl'}, dimensions={0} | all-to-all | bytes 1310720 | tf_op jit(solution)/shard_map/all_to_all | solution.py:556
  108.1 10.1 %all_to_all.22.x_ref = bf16[4,80,128]{2,1,0:T(8,128)(2,1)S(1)} all-to-all(bf16[4,80,128]{2,1,0:T(8,128)(2,1)S(1)} %sum_rows.1), channel_id=1, replica_groups=mesh['yh'=2,'x'=4,'a'=4,'b'=2,'yl'=2,'c'=2] {'a'}, dimensions={0} | all-to-all | bytes 163840 | tf_op jit(solution)/shard_map/all_to_all | solution.py:558
  118.2 13.3 %all_to_all.23.x_ref = bf16[32,64,128]{2,1,0:T(8,128)(2,1)S(1)} all-to-all(bf16[32,64,128]{2,1,0:T(8,128)(2,1)S(1)} %get-tuple-element.76), channel_id=1, replica_groups=mesh['yh'=2,'x'=4,'a'=4,'b'=2,'yl'=2,'c'=2] {'yh','x','b','yl'}, dimensions={0} | all-to-all | bytes 1048576 | tf_op jit(solution)/shard_map/all_to_all | solution.py:562
  131.6 4.4 %collective-permute-start.22 = (bf16[32,64,128]{2,1,0:T(8,128)(2,1)S(1)}, bf16[32,64,128]{2,1,0:T(8,128)(2,1)S(1)}, u32[]{:S(2)}, u32[]{:S(2)}) collective-permute-start(bf16[32,64,128]{2,1,0:T(8,128)(2,1)S(1)} %all_to_all.23.x_ref), channel_id=1, source_target_pairs={{0,1},{1,0},{2,3},{3,2},{4,5},{5,4},{6,7},{7,6},{8,9},{9,8},{10,11... | collective-permute-start | bytes 1572872 | tf_op jit(solution)/shard_map/ppermute | solution.py:441
  136.5 1.7 %unfold.2.refs_0_ = f32[4096,128]{1,0:T(8,128)} custom-call(s32[6]{0:T(128)S(1)} %stack.45.pos_ref, bf16[32,64,128]{2,1,0:T(8,128)(2,1)S(1)} %all_to_all.23.x_ref), custom_call_target="tpu_custom_call" | custom-call | tf_op jit(solution)/shard_map/unfold/pallas_call | solution.py:566
  138.2 1.7 %unfold.3 = f32[4096,128]{1,0:T(8,128)} custom-call(s32[6]{0:T(128)S(1)} %stack.45.pos_ref, bf16[32,64,128]{2,1,0:T(8,128)(2,1)S(1)} %collective-permute-done.22.x_ref, f32[4096,128]{1,0:T(8,128)} %unfold.2.refs_0_), custom_call_target="tpu_custom_call", output_to_operand_aliasing={{}: (2, {})} | custom-call | tf_op jit(solution)/shard_map/unfold/pallas_call | solution.py:566
  (49 shorter events, 5.2 us)
Async XLA Ops:
  6.4 50.8 %copy-start.4 = (f32[8,128]{1,0:T(8,128)S(1)}, f32[8,128]{1,0:T(8,128)}, u32[]{:S(2)}) copy-start(f32[8,128]{1,0:T(8,128)} %get-tuple-element.40.const_ref) | copy-start | bytes 12292
  6.4 8.0 %collective-permute-start = (bf16[304,128]{1,0:T(8,128)(2,1)}, bf16[304,128]{1,0:T(8,128)(2,1)S(1)}, u32[]{:S(2)}, u32[]{:S(2)}) collective-permute-start(bf16[304,128]{1,0:T(8,128)(2,1)} %get-tuple-element.41), channel_id=1, source_target_pairs={{0,8},{8,0},{16,24},{24,16},{1,9},{9,1},{17,25},{25,17},{2,10},{10... | collective-permute-start | bytes 233480 | tf_op jit(solution)/shard_map/ppermute | solution.py:449
  10.3 14.0 %collective-permute-start.5 = (bf16[304,128]{1,0:T(8,128)(2,1)}, bf16[304,128]{1,0:T(8,128)(2,1)S(1)}, u32[]{:S(2)}, u32[]{:S(2)}) collective-permute-start(bf16[304,128]{1,0:T(8,128)(2,1)} %get-tuple-element.44), channel_id=1, source_target_pairs={{0,32},{32,0},{64,96},{96,64},{1,33},{33,1},{65,97},{97,65},{2,34}... | collective-permute-start | bytes 233480 | tf_op jit(solution)/shard_map/ppermute | solution.py:449
  11.5 13.8 %collective-permute-start.11 = (bf16[528,128]{1,0:T(8,128)(2,1)}, bf16[528,128]{1,0:T(8,128)(2,1)S(1)}, u32[]{:S(2)}, u32[]{:S(2)}) collective-permute-start(bf16[528,128]{1,0:T(8,128)(2,1)} %get-tuple-element.42.refs_2_.refs_8_), channel_id=1, source_target_pairs={{0,128},{128,0},{1,129},{129,1},{2,130},{130,2},{3,131},{131,3},{4... | collective-permute-start | bytes 405512 | tf_op jit(solution)/shard_map/ppermute | solution.py:441
  15.3 20.4 %collective-permute-start.1 = (bf16[2,304,128]{2,1,0:T(8,128)(2,1)S(1)}, bf16[2,304,128]{2,1,0:T(8,128)(2,1)S(1)}, u32[]{:S(2)}, u32[]{:S(2)}) collective-permute-start(bf16[2,304,128]{2,1,0:T(8,128)(2,1)S(1)} %pad_maximum_fusion.refs_0_), channel_id=1, source_target_pairs={{0,16},{8,24},{16,0},{24,8},{1,17},{9,25},{17,1},{25,9},{2,18},{10... | collective-permute-start | bytes 466952 | tf_op jit(solution)/shard_map/ppermute | solution.py:449
  21.8 10.0 %collective-permute-start.4 = (bf16[528,128]{1,0:T(8,128)(2,1)}, bf16[528,128]{1,0:T(8,128)(2,1)S(1)}, u32[]{:S(2)}, u32[]{:S(2)}) collective-permute-start(bf16[528,128]{1,0:T(8,128)(2,1)} %get-tuple-element.42.refs_2_.refs_8_), channel_id=1, source_target_pairs={{0,6},{2,4},{4,2},{6,0},{1,7},{3,5},{5,3},{7,1},{8,14},{10,12},{12... | collective-permute-start | bytes 405512 | tf_op jit(solution)/shard_map/ppermute | solution.py:445
  21.8 12.5 %collective-permute-start.3 = (bf16[528,128]{1,0:T(8,128)(2,1)}, bf16[528,128]{1,0:T(8,128)(2,1)S(1)}, u32[]{:S(2)}, u32[]{:S(2)}) collective-permute-start(bf16[528,128]{1,0:T(8,128)(2,1)} %get-tuple-element.42.refs_2_.refs_8_), channel_id=1, source_target_pairs={{0,4},{4,0},{1,5},{5,1},{2,6},{6,2},{3,7},{7,3},{8,12},{12,8},{9,1... | collective-permute-start | bytes 405512 | tf_op jit(solution)/shard_map/ppermute | solution.py:441
  24.2 11.4 %collective-permute-start.2 = (bf16[528,128]{1,0:T(8,128)(2,1)}, bf16[528,128]{1,0:T(8,128)(2,1)S(1)}, u32[]{:S(2)}, u32[]{:S(2)}) collective-permute-start(bf16[528,128]{1,0:T(8,128)(2,1)} %get-tuple-element.42.refs_2_.refs_8_), channel_id=1, source_target_pairs={{0,2},{2,0},{1,3},{3,1},{4,6},{6,4},{5,7},{7,5},{8,10},{10,8},{9,1... | collective-permute-start | bytes 405512 | tf_op jit(solution)/shard_map/ppermute | solution.py:441
  25.3 14.1 %collective-permute-start.6 = (bf16[2,304,128]{2,1,0:T(8,128)(2,1)S(1)}, bf16[2,304,128]{2,1,0:T(8,128)(2,1)S(1)}, u32[]{:S(2)}, u32[]{:S(2)}) collective-permute-start(bf16[2,304,128]{2,1,0:T(8,128)(2,1)S(1)} %pad_maximum_fusion.1.refs_2_), channel_id=1, source_target_pairs={{0,64},{32,96},{64,0},{96,32},{1,65},{33,97},{65,1},{97,33},{2,66}... | collective-permute-start | bytes 466952 | tf_op jit(solution)/shard_map/ppermute | solution.py:449
  31.8 7.7 %collective-permute-start.7 = (bf16[528,128]{1,0:T(8,128)(2,1)}, bf16[528,128]{1,0:T(8,128)(2,1)S(1)}, u32[]{:S(2)}, u32[]{:S(2)}) collective-permute-start(bf16[528,128]{1,0:T(8,128)(2,1)} %get-tuple-element.42.refs_2_.refs_8_), channel_id=1, source_target_pairs={{0,1},{1,0},{2,3},{3,2},{4,5},{5,4},{6,7},{7,6},{8,9},{9,8},{10,11... | collective-permute-start | bytes 405512 | tf_op jit(solution)/shard_map/ppermute | solution.py:441
  34.3 5.2 %collective-permute-start.10 = (bf16[528,128]{1,0:T(8,128)(2,1)S(1)}, bf16[528,128]{1,0:T(8,128)(2,1)S(1)}, u32[]{:S(2)}, u32[]{:S(2)}) collective-permute-start(bf16[528,128]{1,0:T(8,128)(2,1)S(1)} %collective-permute-done.4.refs_5_), channel_id=1, source_target_pairs={{0,1},{1,0},{2,3},{3,2},{4,5},{5,4},{6,7},{7,6},{8,9},{9,8},{10,11... | collective-permute-start | bytes 405512 | tf_op jit(solution)/shard_map/ppermute | solution.py:441
  35.7 3.8 %collective-permute-start.9 = (bf16[528,128]{1,0:T(8,128)(2,1)S(1)}, bf16[528,128]{1,0:T(8,128)(2,1)S(1)}, u32[]{:S(2)}, u32[]{:S(2)}) collective-permute-start(bf16[528,128]{1,0:T(8,128)(2,1)S(1)} %collective-permute-done.3.refs_4_), channel_id=1, source_target_pairs={{0,1},{1,0},{2,3},{3,2},{4,5},{5,4},{6,7},{7,6},{8,9},{9,8},{10,11... | collective-permute-start | bytes 405512 | tf_op jit(solution)/shard_map/ppermute | solution.py:441
  35.7 3.8 %collective-permute-start.8 = (bf16[528,128]{1,0:T(8,128)(2,1)S(1)}, bf16[528,128]{1,0:T(8,128)(2,1)S(1)}, u32[]{:S(2)}, u32[]{:S(2)}) collective-permute-start(bf16[528,128]{1,0:T(8,128)(2,1)S(1)} %collective-permute-done.2.refs_3_), channel_id=1, source_target_pairs={{0,1},{1,0},{2,3},{3,2},{4,5},{5,4},{6,7},{7,6},{8,9},{9,8},{10,11... | collective-permute-start | bytes 405512 | tf_op jit(solution)/shard_map/ppermute | solution.py:441
  36.3 0.9 copy-start.2
  62.1 8.2 %collective-permute-start.12 = (bf16[4,512,128]{2,1,0:T(8,128)(2,1)S(1)}, bf16[4,512,128]{2,1,0:T(8,128)(2,1)S(1)}, u32[]{:S(2)}, u32[]{:S(2)}) collective-permute-start(bf16[4,512,128]{2,1,0:T(8,128)(2,1)S(1)} %get-tuple-element.60), channel_id=1, source_target_pairs={{0,1},{1,0},{2,3},{3,2},{4,5},{5,4},{6,7},{7,6},{8,9},{9,8},{10,11... | collective-permute-start | bytes 1572872 | tf_op jit(solution)/shard_map/ppermute | solution.py:441
  63.9 20.2 %copy-start = (bf16[4,128,4096]{2,1,0:T(8,128)(2,1)S(1)}, bf16[4,128,4096]{2,1,0:T(8,128)(2,1)}, u32[]{:S(2)}) copy-start(bf16[4,128,4096]{2,1,0:T(8,128)(2,1)} %param.9) | copy-start | bytes 12582916
  63.9 20.2 %copy-start.3 = (f32[768,128]{1,0:T(8,128)S(1)}, f32[768,128]{1,0:T(8,128)}, u32[]{:S(2)}) copy-start(f32[768,128]{1,0:T(8,128)} %get-tuple-element.54.raw_ref) | copy-start | bytes 1179652
  65.8 18.3 %copy-start.1 = (bf16[8,32,4096]{2,1,0:T(8,128)(2,1)S(1)}, bf16[8,32,4096]{2,1,0:T(8,128)(2,1)}, u32[]{:S(2)}) copy-start(bf16[8,32,4096]{2,1,0:T(8,128)(2,1)} %param.8) | copy-start | bytes 6291460
  65.8 18.3 %copy-start.5 = (s32[4]{0:T(128)S(1)}, s32[4]{0:T(128)}, u32[]{:S(2)}) copy-start(s32[4]{0:T(128)} %p_len_ref.3) | copy-start | bytes 52
  65.8 9.4 %collective-permute-start.15 = (bf16[2,256,128]{2,1,0:T(8,128)(2,1)S(1)}, bf16[2,256,128]{2,1,0:T(8,128)(2,1)S(1)}, u32[]{:S(2)}, u32[]{:S(2)}) collective-permute-start(bf16[2,256,128]{2,1,0:T(8,128)(2,1)S(1)} %get-tuple-element.67), channel_id=1, source_target_pairs={{0,16},{8,24},{16,0},{24,8},{1,17},{9,25},{17,1},{25,9},{2,18},{10... | collective-permute-start | bytes 393224 | tf_op jit(solution)/shard_map/ppermute | solution.py:449
  66.4 13.1 %collective-permute-start.13 = (bf16[2,256,128]{2,1,0:T(8,128)(2,1)S(1)}, bf16[2,256,128]{2,1,0:T(8,128)(2,1)S(1)}, u32[]{:S(2)}, u32[]{:S(2)}) collective-permute-start(bf16[2,256,128]{2,1,0:T(8,128)(2,1)S(1)} %get-tuple-element.63), channel_id=1, source_target_pairs={{0,64},{32,96},{64,0},{96,32},{1,65},{33,97},{65,1},{97,33},{2,66}... | collective-permute-start | bytes 393224 | tf_op jit(solution)/shard_map/ppermute | solution.py:449
  67.4 12.3 %collective-permute-start.20 = (bf16[512,128]{1,0:T(8,128)(2,1)S(1)}, bf16[512,128]{1,0:T(8,128)(2,1)S(1)}, u32[]{:S(2)}, u32[]{:S(2)}) collective-permute-start(bf16[512,128]{1,0:T(8,128)(2,1)S(1)} %get-tuple-element.73), channel_id=1, source_target_pairs={{0,128},{128,0},{1,129},{129,1},{2,130},{130,2},{3,131},{131,3},{4... | collective-permute-start | bytes 393224 | tf_op jit(solution)/shard_map/ppermute | solution.py:441
  70.4 13.6 %collective-permute-start.17 = (bf16[512,128]{1,0:T(8,128)(2,1)S(1)}, bf16[512,128]{1,0:T(8,128)(2,1)S(1)}, u32[]{:S(2)}, u32[]{:S(2)}) collective-permute-start(bf16[512,128]{1,0:T(8,128)(2,1)S(1)} %get-tuple-element.70), channel_id=1, source_target_pairs={{0,2},{2,0},{1,3},{3,1},{4,6},{6,4},{5,7},{7,5},{8,10},{10,8},{9,1... | collective-permute-start | bytes 393224 | tf_op jit(solution)/shard_map/ppermute | solution.py:441
  70.9 13.1 %collective-permute-start.18 = (bf16[512,128]{1,0:T(8,128)(2,1)S(1)}, bf16[512,128]{1,0:T(8,128)(2,1)S(1)}, u32[]{:S(2)}, u32[]{:S(2)}) collective-permute-start(bf16[512,128]{1,0:T(8,128)(2,1)S(1)} %get-tuple-element.71), channel_id=1, source_target_pairs={{0,4},{4,0},{1,5},{5,1},{2,6},{6,2},{3,7},{7,3},{8,12},{12,8},{9,1... | collective-permute-start | bytes 393224 | tf_op jit(solution)/shard_map/ppermute | solution.py:441
  75.2 8.8 %collective-permute-start.19 = (bf16[512,128]{1,0:T(8,128)(2,1)S(1)}, bf16[512,128]{1,0:T(8,128)(2,1)S(1)}, u32[]{:S(2)}, u32[]{:S(2)}) collective-permute-start(bf16[512,128]{1,0:T(8,128)(2,1)S(1)} %get-tuple-element.72), channel_id=1, source_target_pairs={{0,6},{2,4},{4,2},{6,0},{1,7},{3,5},{5,3},{7,1},{8,14},{10,12},{12... | collective-permute-start | bytes 393224 | tf_op jit(solution)/shard_map/ppermute | solution.py:445
  79.6 4.4 %collective-permute-start.16 = (bf16[256,128]{1,0:T(8,128)(2,1)S(1)}, bf16[256,128]{1,0:T(8,128)(2,1)S(1)}, u32[]{:S(2)}, u32[]{:S(2)}) collective-permute-start(bf16[256,128]{1,0:T(8,128)(2,1)S(1)} %get-tuple-element.69), channel_id=1, source_target_pairs={{0,8},{8,0},{16,24},{24,16},{1,9},{9,1},{17,25},{25,17},{2,10},{10... | collective-permute-start | bytes 196616 | tf_op jit(solution)/shard_map/ppermute | solution.py:449
  79.7 4.3 %collective-permute-start.14 = (bf16[256,128]{1,0:T(8,128)(2,1)S(1)}, bf16[256,128]{1,0:T(8,128)(2,1)S(1)}, u32[]{:S(2)}, u32[]{:S(2)}) collective-permute-start(bf16[256,128]{1,0:T(8,128)(2,1)S(1)} %get-tuple-element.65), channel_id=1, source_target_pairs={{0,32},{32,0},{64,96},{96,64},{1,33},{33,1},{65,97},{97,65},{2,34}... | collective-permute-start | bytes 196616 | tf_op jit(solution)/shard_map/ppermute | solution.py:449
  86.7 4.5 %collective-permute-start.21 = (bf16[32,80,128]{2,1,0:T(8,128)(2,1)S(1)}, bf16[32,80,128]{2,1,0:T(8,128)(2,1)S(1)}, u32[]{:S(2)}, u32[]{:S(2)}) collective-permute-start(bf16[32,80,128]{2,1,0:T(8,128)(2,1)S(1)} %get-tuple-element.75), channel_id=1, source_target_pairs={{0,1},{1,0},{2,3},{3,2},{4,5},{5,4},{6,7},{7,6},{8,9},{9,8},{10,11... | collective-permute-start | bytes 1966088 | tf_op jit(solution)/shard_map/ppermute | solution.py:441
  131.6 6.6 %collective-permute-start.22 = (bf16[32,64,128]{2,1,0:T(8,128)(2,1)S(1)}, bf16[32,64,128]{2,1,0:T(8,128)(2,1)S(1)}, u32[]{:S(2)}, u32[]{:S(2)}) collective-permute-start(bf16[32,64,128]{2,1,0:T(8,128)(2,1)S(1)} %all_to_all.23.x_ref), channel_id=1, source_target_pairs={{0,1},{1,0},{2,3},{3,2},{4,5},{5,4},{6,7},{7,6},{8,9},{9,8},{10,11... | collective-permute-start | bytes 1572872 | tf_op jit(solution)/shard_map/ppermute | solution.py:441

commit v2 on v1

--- a/solution.py
+++ b/solution.py
@@ -449,8 +449,27 @@
     return lax.ppermute(x, axis, [(i, i ^ d) for i in range(4)])
 
 
+def stack_two(x_ref, y_ref, out_ref, sems):
+    copies = [pltpu.make_async_copy(r, out_ref.at[k], sems.at[k]) for k, r in enumerate((x_ref, y_ref))]
+    for copy in copies:
+        copy.start()
+    for copy in copies:
+        copy.wait()
+
+
+def stacked(x, y):
+    return pl.pallas_call(
+        stack_two,
+        in_specs=[ANY, ANY],
+        out_specs=VMEM,
+        out_shape=sds((2, *x.shape), x.dtype),
+        scratch_shapes=[pltpu.SemaphoreType.DMA((2,))],
+        name="stack_two",
+    )(x, y)
+
+
 def doubled(x, axis):
-    pair = jnp.stack([x, swap(x, axis, 1)])
+    pair = stacked(x, swap(x, axis, 1))
     return [pair, swap(pair, axis, 2)]
 
 

time: 140 us -> 145 us (1.036)
  local copies, waits for them, and re-layouts: 1.53 us -> 6.26 us
  Pallas kernels: 26.8 us -> 29.8 us
  other arithmetic: 2.01 us -> 0.17 us
  waiting for transfers between devices: 11.8 us -> 10.3 us
    unnamed x12 -> x30, local copies, waits for them, and re-layouts: 0.93 us -> 5.67 us
    pallas_call x0 -> x2, Pallas kernels: none -> 3.21 us  [stacked(): pl.pallas_call(stack_two, in_specs=[ANY, ANY], out_specs=VMEM, out_shape=...]
    another operation x2 -> x0, other arithmetic: 1.8 us -> none  [doubled(): pair = jnp.stack([x, swap(x, axis, 1)])]
  transfers between devices with their start and end apart: 23 -> 23, of which waited for: 5 -> 4; matrix products, arithmetic and copies ran while one was open for 2% -> 0% of each run, Pallas kernels for 5% -> 7%
where the time goes in v2:
time: 145 us
  blocking collectives  53.5 us (37%)
  starting transfers between devices  44 us (30%)
  Pallas kernels  29.8 us (21%)
  waiting for transfers between devices  10.3 us (7%)
  local copies, waits for them, and re-layouts  6.26 us (4%)
    all_to_all x2, blocking collectives, local(): part = lax.all_to_all(part, SCATTER, 0, 0, tiled=True)  29.7 us
    ppermute x13, starting transfers between devices, flip(): return lax.ppermute(x, axis, [(0, 1), (1, 0)])  23.4 us
    ppermute x8, starting transfers between devices, swap(): return lax.ppermute(x, axis, [(i, i ^ d) for i in range(4)])  16.2 us
    all_to_all x1, blocking collectives, local(): rows = lax.all_to_all(rows, ('x', 'a'), 0, 0, tiled=True)  13.7 us
    all_to_all x1, blocking collectives, local(): part = lax.all_to_all(part, 'a', 0, 0, tiled=True)  10.1 us
    ppermute x8, waiting for transfers between devices, swap(): return lax.ppermute(x, axis, [(i, i ^ d) for i in range(4)])  7.9 us
    pallas_call x1, Pallas kernels, local(): pl.pallas_call(project, in_specs=[SMEM] * 3 + [ANY] * 5, out_specs=[VMEM]...  5.72 us
    unnamed x30, local copies, waits for them, and re-layouts  5.67 us
  transfers between devices with their start and end apart: 23, of which 4 were waited for; matrix products, arithmetic and copies ran while one was open for 0% of the time, Pallas kernels for 7%

profile of v2, /device:TPU:1, one launch (start us, length us, event | category | flops | bytes accessed | tf_op | source)
XLA Modules:
  0.0 145.0 jit_solution(14380562887220142732)
XLA Ops:
  0.6 5.7 %project.1 = (f32[768,128]{1,0:T(8,128)}, bf16[528,128]{1,0:T(8,128)(2,1)}, bf16[304,128]{1,0:T(8,128)(2,1)}, bf16[304,128]{1,0:T(8,128)(2,1)}, f32[8,128]{1,0:T(8,128)}) custom-call(s32[8]{0:T(128)} %q_len_ref.1, s32[4]{0:T(128)} %p_len_ref.3, s32[8]{0:T(128)} %count_ref.1, bf16[256,4096]{1,0:T(8,128)(2,1)} %bitcast.12, bf16[512,4096]{1,0:T(8,128)(2,1)} %bitcast.9, ...), custom_call_target="tpu_custom_call" | custom-call | tf_op jit(solution)/shard_map/project/pallas_call | solution.py:481
  6.4 3.9 %collective-permute-start = (bf16[304,128]{1,0:T(8,128)(2,1)}, bf16[304,128]{1,0:T(8,128)(2,1)S(1)}, u32[]{:S(2)}, u32[]{:S(2)}) collective-permute-start(bf16[304,128]{1,0:T(8,128)(2,1)} %get-tuple-element.41.x_ref), channel_id=1, source_target_pairs={{0,8},{8,0},{16,24},{24,16},{1,9},{9,1},{17,25},{25,17},{2,10},{10... | collective-permute-start | bytes 233480 | tf_op jit(solution)/shard_map/ppermute | solution.py:449
  10.3 1.2 collective-permute-start.5
  11.5 2.9 %collective-permute-start.11 = (bf16[528,128]{1,0:T(8,128)(2,1)}, bf16[528,128]{1,0:T(8,128)(2,1)S(1)}, u32[]{:S(2)}, u32[]{:S(2)}) collective-permute-start(bf16[528,128]{1,0:T(8,128)(2,1)} %get-tuple-element.42.refs_2_.refs_8_), channel_id=1, source_target_pairs={{0,128},{128,0},{1,129},{129,1},{2,130},{130,2},{3,131},{131,3},{4... | collective-permute-start | bytes 405512 | tf_op jit(solution)/shard_map/ppermute | solution.py:441
  15.0 1.6 %stack_two.2.refs_0_ = bf16[2,304,128]{2,1,0:T(8,128)(2,1)} custom-call(bf16[304,128]{1,0:T(8,128)(2,1)} %get-tuple-element.41.x_ref, bf16[304,128]{1,0:T(8,128)(2,1)} %copy-done.14), custom_call_target="tpu_custom_call" | custom-call | tf_op jit(solution)/shard_map/stack_two/pallas_call | solution.py:461
  16.7 6.4 %collective-permute-start.1 = (bf16[2,304,128]{2,1,0:T(8,128)(2,1)}, bf16[2,304,128]{2,1,0:T(8,128)(2,1)S(1)}, u32[]{:S(2)}, u32[]{:S(2)}) collective-permute-start(bf16[2,304,128]{2,1,0:T(8,128)(2,1)} %stack_two.2.refs_0_), channel_id=1, source_target_pairs={{0,16},{8,24},{16,0},{24,8},{1,17},{9,25},{17,1},{25,9},{2,18},{10... | collective-permute-start | bytes 466952 | tf_op jit(solution)/shard_map/ppermute | solution.py:449
  23.1 2.5 %collective-permute-start.3 = (bf16[528,128]{1,0:T(8,128)(2,1)}, bf16[528,128]{1,0:T(8,128)(2,1)S(1)}, u32[]{:S(2)}, u32[]{:S(2)}) collective-permute-start(bf16[528,128]{1,0:T(8,128)(2,1)} %get-tuple-element.42.refs_2_.refs_8_), channel_id=1, source_target_pairs={{0,4},{4,0},{1,5},{5,1},{2,6},{6,2},{3,7},{7,3},{8,12},{12,8},{9,1... | collective-permute-start | bytes 405512 | tf_op jit(solution)/shard_map/ppermute | solution.py:441
  26.2 1.6 %stack_two.3.refs_2_ = bf16[2,304,128]{2,1,0:T(8,128)(2,1)} custom-call(bf16[304,128]{1,0:T(8,128)(2,1)} %get-tuple-element.44.x_ref, bf16[304,128]{1,0:T(8,128)(2,1)} %copy-done.13), custom_call_target="tpu_custom_call" | custom-call | tf_op jit(solution)/shard_map/stack_two/pallas_call | solution.py:461
  27.9 2.8 %collective-permute-start.6 = (bf16[2,304,128]{2,1,0:T(8,128)(2,1)}, bf16[2,304,128]{2,1,0:T(8,128)(2,1)S(1)}, u32[]{:S(2)}, u32[]{:S(2)}) collective-permute-start(bf16[2,304,128]{2,1,0:T(8,128)(2,1)} %stack_two.3.refs_2_), channel_id=1, source_target_pairs={{0,64},{32,96},{64,0},{96,32},{1,65},{33,97},{65,1},{97,33},{2,66}... | collective-permute-start | bytes 466952 | tf_op jit(solution)/shard_map/ppermute | solution.py:449
  30.7 2.2 %collective-permute-done.4.refs_5_ = bf16[528,128]{1,0:T(8,128)(2,1)S(1)} collective-permute-done((bf16[528,128]{1,0:T(8,128)(2,1)}, bf16[528,128]{1,0:T(8,128)(2,1)S(1)}, u32[]{:S(2)}, u32[]{:S(2)}) %collective-permute-start.4) | collective-permute-done | bytes 135200 | tf_op jit(solution)/shard_map/ppermute | solution.py:445
  32.9 2.9 %collective-permute-start.7 = (bf16[528,128]{1,0:T(8,128)(2,1)}, bf16[528,128]{1,0:T(8,128)(2,1)S(1)}, u32[]{:S(2)}, u32[]{:S(2)}) collective-permute-start(bf16[528,128]{1,0:T(8,128)(2,1)} %get-tuple-element.42.refs_2_.refs_8_), channel_id=1, source_target_pairs={{0,1},{1,0},{2,3},{3,2},{4,5},{5,4},{6,7},{7,6},{8,9},{9,8},{10,11... | collective-permute-start | bytes 405512 | tf_op jit(solution)/shard_map/ppermute | solution.py:441
  35.9 1.3 collective-permute-start.10
  39.6 2.3 %forward_first.1 = (f32[4,512,1024]{2,1,0:T(8,128)S(1)}, f32[16,1024]{1,0:T(8,128)S(1)}, f32[16,32]{1,0:T(8,128)S(1)}) custom-call(s32[6]{0:T(128)S(1)} %stack.27.pos_ref, bf16[2,304,128]{2,1,0:T(8,128)(2,1)S(1)} %copy-done.2, bf16[2,304,128]{2,1,0:T(8,128)(2,1)S(1)} %collective-permute-done.1.refs_1_, bf16[528,128]{1,0:T(8,128)(2,1)S(1)} %copy-done.5, ...), custom_call_target="tpu_custom_call" | custom-call | tf_op jit(solution)/shard_map/forward_first/pallas_call | solution.py:502
  44.7 3.9 %forward_second.1 = (f32[4,512,1024]{2,1,0:T(8,128)S(1)}, f32[16,1024]{1,0:T(8,128)S(1)}, f32[16,32]{1,0:T(8,128)S(1)}, f32[2,512,1024]{2,1,0:T(8,128)S(1)}, f32...) custom-call(s32[6]{0:T(128)S(1)} %stack.27.pos_ref, ...), custom_call_target="tpu_custom_call" | custom-call | tf_op jit(solution)/shard_map/forward_second/pallas_call | solution.py:507
  48.6 13.7 %all_to_all.20.rows_ref = f32[16,8,128]{2,1,0:T(8,128)S(1)} all-to-all(f32[16,8,128]{2,1,0:T(8,128)S(1)} %get-tuple-element.45), channel_id=1, replica_groups=mesh['yh'=2,'x'=4,'a'=4,'b'=2,'yl'=2,'c'=2] {'x','a'}, dimensions={0} | all-to-all | bytes 131072 | tf_op jit(solution)/shard_map/all_to_all | solution.py:514
  62.3 4.9 %backward_first.1 = (bf16[4,512,128]{2,1,0:T(8,128)(2,1)S(1)}, bf16[512,128]{1,0:T(8,128)(2,1)S(1)}, bf16[2,256,128]{2,1,0:T(8,128)(2,1)S(1)}, f32[2,256,128]{2,...) custom-call(s32[6]{0:T(128)S(1)} %stack.27.pos_ref, ...), custom_call_target="tpu_custom_call" | custom-call | tf_op jit(solution)/shard_map/backward_first/pallas_call | solution.py:516
  67.2 1.8 %collective-permute-start.12 = (bf16[4,512,128]{2,1,0:T(8,128)(2,1)S(1)}, bf16[4,512,128]{2,1,0:T(8,128)(2,1)S(1)}, u32[]{:S(2)}, u32[]{:S(2)}) collective-permute-start(bf16[4,512,128]{2,1,0:T(8,128)(2,1)S(1)} %get-tuple-element.60), channel_id=1, source_target_pairs={{0,1},{1,0},{2,3},{3,2},{4,5},{5,4},{6,7},{7,6},{8,9},{9,8},{10,11... | collective-permute-start | bytes 1572872 | tf_op jit(solution)/shard_map/ppermute | solution.py:441
  69.0 1.9 %backward_second.1 = (f32[2,256,128]{2,1,0:T(8,128)S(1)}, bf16[2,256,128]{2,1,0:T(8,128)(2,1)S(1)}, f32[4,512,128]{2,1,0:T(8,128)S(1)}) custom-call(f32[16,1024]{1,0:T(8,128)S(1)} %get-tuple-element.55.coef_ref, f32[128,1024]{1,0:T(8,128)S(1)} %get-tuple-element.56.q_part, f32[512,128]{1,0:T(8,128)S(1)} %get-tuple-element.57.p_part, ...), custom_call_target="tpu_custom_call" | custom-call | tf_op jit(solution)/shard_map/backward_second/pallas_call | solution.py:525
  71.6 0.9 collective-permute-start.13
  72.5 2.9 %collective-permute-start.20 = (bf16[512,128]{1,0:T(8,128)(2,1)S(1)}, bf16[512,128]{1,0:T(8,128)(2,1)S(1)}, u32[]{:S(2)}, u32[]{:S(2)}) collective-permute-start(bf16[512,128]{1,0:T(8,128)(2,1)S(1)} %get-tuple-element.73), channel_id=1, source_target_pairs={{0,128},{128,0},{1,129},{129,1},{2,130},{130,2},{3,131},{131,3},{4... | collective-permute-start | bytes 393224 | tf_op jit(solution)/shard_map/ppermute | solution.py:441
  76.6 3.8 %collective-permute-done.15.more_ref = bf16[2,256,128]{2,1,0:T(8,128)(2,1)S(1)} collective-permute-done((bf16[2,256,128]{2,1,0:T(8,128)(2,1)S(1)}, bf16[2,256,128]{2,1,0:T(8,128)(2,1)S(1)}, u32[]{:S(2)}, u32[]{:S(2)}) %collective-permute-start.15) | collective-permute-done | bytes 131104 | tf_op jit(solution)/shard_map/ppermute | solution.py:449
  80.4 4.3 %collective-permute-start.19 = (bf16[512,128]{1,0:T(8,128)(2,1)S(1)}, bf16[512,128]{1,0:T(8,128)(2,1)S(1)}, u32[]{:S(2)}, u32[]{:S(2)}) collective-permute-start(bf16[512,128]{1,0:T(8,128)(2,1)S(1)} %get-tuple-element.72), channel_id=1, source_target_pairs={{0,6},{2,4},{4,2},{6,0},{1,7},{3,5},{5,3},{7,1},{8,14},{10,12},{12... | collective-permute-start | bytes 393224 | tf_op jit(solution)/shard_map/ppermute | solution.py:445
  85.0 4.1 %collective-permute-done.16.refs_3_ = bf16[256,128]{1,0:T(8,128)(2,1)S(1)} collective-permute-done((bf16[256,128]{1,0:T(8,128)(2,1)S(1)}, bf16[256,128]{1,0:T(8,128)(2,1)S(1)}, u32[]{:S(2)}, u32[]{:S(2)}) %collective-permute-start.16) | collective-permute-done | bytes 65568 | tf_op jit(solution)/shard_map/ppermute | solution.py:449
  89.2 2.6 %finish.1 = (bf16[32,80,128]{2,1,0:T(8,128)(2,1)S(1)}, bf16[128,768]{1,0:T(8,128)(2,1)S(1)}) custom-call(s32[6]{0:T(128)S(1)} %stack.27.pos_ref, s32[4]{0:T(128)S(1)} %copy-done.12, bf16[256,4096]{1,0:T(8,128)(2,1)S(1)} %bitcast.13, bf16[512,4096]{1,0:T(8,128)(2,1)S(1)} %bitcast.10, f32[8,128]{1,0:T(8,128)S(1)} %get-tuple-element.53.loss_ref, ...), custom_call_target="tpu_custom_call" | custom-call | tf_op jit(solution)/shard_map/finish/pallas_call | solution.py:565
  91.9 2.8 %collective-permute-start.21 = (bf16[32,80,128]{2,1,0:T(8,128)(2,1)S(1)}, bf16[32,80,128]{2,1,0:T(8,128)(2,1)S(1)}, u32[]{:S(2)}, u32[]{:S(2)}) collective-permute-start(bf16[32,80,128]{2,1,0:T(8,128)(2,1)S(1)} %get-tuple-element.75), channel_id=1, source_target_pairs={{0,1},{1,0},{2,3},{3,2},{4,5},{5,4},{6,7},{7,6},{8,9},{9,8},{10,11... | collective-permute-start | bytes 1966088 | tf_op jit(solution)/shard_map/ppermute | solution.py:441
  94.7 1.6 %finish_more.1 = bf16[32,80,128]{2,1,0:T(8,128)(2,1)S(1)} custom-call(s32[6]{0:T(128)S(1)} %stack.27.pos_ref, bf16[256,4096]{1,0:T(8,128)(2,1)S(1)} %bitcast.14, bf16[512,4096]{1,0:T(8,128)(2,1)S(1)} %bitcast.11, f32[8,128]{1,0:T(8,128)S(1)} %get-tuple-element.53.loss_ref, bf16[128,768]{1,0:T(8,128)(2,1)S(1)} %get-tuple-element.74.backs_ref), custom_call_target="tpu_custom_call" | custom-call | tf_op jit(solution)/shard_map/finish_more/pallas_call | solution.py:570
  96.6 16.4 %all_to_all.21.x_ref = bf16[32,80,128]{2,1,0:T(8,128)(2,1)S(1)} all-to-all(bf16[32,80,128]{2,1,0:T(8,128)(2,1)S(1)} %add_convert_fusion), channel_id=1, replica_groups=mesh['yh'=2,'x'=4,'a'=4,'b'=2,'yl'=2,'c'=2] {'yh','x','b','yl'}, dimensions={0} | all-to-all | bytes 1310720 | tf_op jit(solution)/shard_map/all_to_all | solution.py:575
  113.1 10.1 %all_to_all.22.x_ref = bf16[4,80,128]{2,1,0:T(8,128)(2,1)S(1)} all-to-all(bf16[4,80,128]{2,1,0:T(8,128)(2,1)S(1)} %sum_rows.1), channel_id=1, replica_groups=mesh['yh'=2,'x'=4,'a'=4,'b'=2,'yl'=2,'c'=2] {'a'}, dimensions={0} | all-to-all | bytes 163840 | tf_op jit(solution)/shard_map/all_to_all | solution.py:577
  123.3 13.3 %all_to_all.23.x_ref = bf16[32,64,128]{2,1,0:T(8,128)(2,1)S(1)} all-to-all(bf16[32,64,128]{2,1,0:T(8,128)(2,1)S(1)} %get-tuple-element.76), channel_id=1, replica_groups=mesh['yh'=2,'x'=4,'a'=4,'b'=2,'yl'=2,'c'=2] {'yh','x','b','yl'}, dimensions={0} | all-to-all | bytes 1048576 | tf_op jit(solution)/shard_map/all_to_all | solution.py:581
  136.7 4.4 %collective-permute-start.22 = (bf16[32,64,128]{2,1,0:T(8,128)(2,1)S(1)}, bf16[32,64,128]{2,1,0:T(8,128)(2,1)S(1)}, u32[]{:S(2)}, u32[]{:S(2)}) collective-permute-start(bf16[32,64,128]{2,1,0:T(8,128)(2,1)S(1)} %all_to_all.23.x_ref), channel_id=1, source_target_pairs={{0,1},{1,0},{2,3},{3,2},{4,5},{5,4},{6,7},{7,6},{8,9},{9,8},{10,11... | collective-permute-start | bytes 1572872 | tf_op jit(solution)/shard_map/ppermute | solution.py:441
  141.6 1.7 %unfold.2.refs_0_ = f32[4096,128]{1,0:T(8,128)} custom-call(s32[6]{0:T(128)S(1)} %stack.27.pos_ref, bf16[32,64,128]{2,1,0:T(8,128)(2,1)S(1)} %all_to_all.23.x_ref), custom_call_target="tpu_custom_call" | custom-call | tf_op jit(solution)/shard_map/unfold/pallas_call | solution.py:585
  143.3 1.7 %unfold.3 = f32[4096,128]{1,0:T(8,128)} custom-call(s32[6]{0:T(128)S(1)} %stack.27.pos_ref, bf16[32,64,128]{2,1,0:T(8,128)(2,1)S(1)} %collective-permute-done.22.x_ref, f32[4096,128]{1,0:T(8,128)} %unfold.2.refs_0_), custom_call_target="tpu_custom_call", output_to_operand_aliasing={{}: (2, {})} | custom-call | tf_op jit(solution)/shard_map/unfold/pallas_call | solution.py:585
  (67 shorter events, 9.6 us)
Async XLA Ops:
  6.4 55.9 %copy-start.7 = (bf16[528,128]{1,0:T(8,128)(2,1)S(1)}, bf16[528,128]{1,0:T(8,128)(2,1)}, u32[]{:S(2)}) copy-start(bf16[528,128]{1,0:T(8,128)(2,1)} %get-tuple-element.42.refs_2_.refs_8_) | copy-start | bytes 405508
  6.4 55.9 %copy-start.11 = (f32[8,128]{1,0:T(8,128)S(1)}, f32[8,128]{1,0:T(8,128)}, u32[]{:S(2)}) copy-start(f32[8,128]{1,0:T(8,128)} %get-tuple-element.40.const_ref) | copy-start | bytes 12292
  6.4 8.0 %collective-permute-start = (bf16[304,128]{1,0:T(8,128)(2,1)}, bf16[304,128]{1,0:T(8,128)(2,1)S(1)}, u32[]{:S(2)}, u32[]{:S(2)}) collective-permute-start(bf16[304,128]{1,0:T(8,128)(2,1)} %get-tuple-element.41.x_ref), channel_id=1, source_target_pairs={{0,8},{8,0},{16,24},{24,16},{1,9},{9,1},{17,25},{25,17},{2,10},{10... | collective-permute-start | bytes 233480 | tf_op jit(solution)/shard_map/ppermute | solution.py:449
  10.3 15.3 %collective-permute-start.5 = (bf16[304,128]{1,0:T(8,128)(2,1)}, bf16[304,128]{1,0:T(8,128)(2,1)S(1)}, u32[]{:S(2)}, u32[]{:S(2)}) collective-permute-start(bf16[304,128]{1,0:T(8,128)(2,1)} %get-tuple-element.44.x_ref), channel_id=1, source_target_pairs={{0,32},{32,0},{64,96},{96,64},{1,33},{33,1},{65,97},{97,65},{2,34}... | collective-permute-start | bytes 233480 | tf_op jit(solution)/shard_map/ppermute | solution.py:449
  11.5 16.3 %collective-permute-start.11 = (bf16[528,128]{1,0:T(8,128)(2,1)}, bf16[528,128]{1,0:T(8,128)(2,1)S(1)}, u32[]{:S(2)}, u32[]{:S(2)}) collective-permute-start(bf16[528,128]{1,0:T(8,128)(2,1)} %get-tuple-element.42.refs_2_.refs_8_), channel_id=1, source_target_pairs={{0,128},{128,0},{1,129},{129,1},{2,130},{130,2},{3,131},{131,3},{4... | collective-permute-start | bytes 405512 | tf_op jit(solution)/shard_map/ppermute | solution.py:441
  16.7 45.6 %copy-start.4 = (bf16[2,304,128]{2,1,0:T(8,128)(2,1)S(1)}, bf16[2,304,128]{2,1,0:T(8,128)(2,1)}, u32[]{:S(2)}) copy-start(bf16[2,304,128]{2,1,0:T(8,128)(2,1)} %stack_two.2.refs_0_) | copy-start | bytes 466948
  16.7 20.6 %collective-permute-start.1 = (bf16[2,304,128]{2,1,0:T(8,128)(2,1)}, bf16[2,304,128]{2,1,0:T(8,128)(2,1)S(1)}, u32[]{:S(2)}, u32[]{:S(2)}) collective-permute-start(bf16[2,304,128]{2,1,0:T(8,128)(2,1)} %stack_two.2.refs_0_), channel_id=1, source_target_pairs={{0,16},{8,24},{16,0},{24,8},{1,17},{9,25},{17,1},{25,9},{2,18},{10... | collective-permute-start | bytes 466952 | tf_op jit(solution)/shard_map/ppermute | solution.py:449
  23.1 9.8 %collective-permute-start.4 = (bf16[528,128]{1,0:T(8,128)(2,1)}, bf16[528,128]{1,0:T(8,128)(2,1)S(1)}, u32[]{:S(2)}, u32[]{:S(2)}) collective-permute-start(bf16[528,128]{1,0:T(8,128)(2,1)} %get-tuple-element.42.refs_2_.refs_8_), channel_id=1, source_target_pairs={{0,6},{2,4},{4,2},{6,0},{1,7},{3,5},{5,3},{7,1},{8,14},{10,12},{12... | collective-permute-start | bytes 405512 | tf_op jit(solution)/shard_map/ppermute | solution.py:445
  23.1 12.8 %collective-permute-start.3 = (bf16[528,128]{1,0:T(8,128)(2,1)}, bf16[528,128]{1,0:T(8,128)(2,1)S(1)}, u32[]{:S(2)}, u32[]{:S(2)}) collective-permute-start(bf16[528,128]{1,0:T(8,128)(2,1)} %get-tuple-element.42.refs_2_.refs_8_), channel_id=1, source_target_pairs={{0,4},{4,0},{1,5},{5,1},{2,6},{6,2},{3,7},{7,3},{8,12},{12,8},{9,1... | collective-permute-start | bytes 405512 | tf_op jit(solution)/shard_map/ppermute | solution.py:441
  25.6 11.6 %collective-permute-start.2 = (bf16[528,128]{1,0:T(8,128)(2,1)}, bf16[528,128]{1,0:T(8,128)(2,1)S(1)}, u32[]{:S(2)}, u32[]{:S(2)}) collective-permute-start(bf16[528,128]{1,0:T(8,128)(2,1)} %get-tuple-element.42.refs_2_.refs_8_), channel_id=1, source_target_pairs={{0,2},{2,0},{1,3},{3,1},{4,6},{6,4},{5,7},{7,5},{8,10},{10,8},{9,1... | collective-permute-start | bytes 405512 | tf_op jit(solution)/shard_map/ppermute | solution.py:441
  27.9 14.1 %collective-permute-start.6 = (bf16[2,304,128]{2,1,0:T(8,128)(2,1)}, bf16[2,304,128]{2,1,0:T(8,128)(2,1)S(1)}, u32[]{:S(2)}, u32[]{:S(2)}) collective-permute-start(bf16[2,304,128]{2,1,0:T(8,128)(2,1)} %stack_two.3.refs_2_), channel_id=1, source_target_pairs={{0,64},{32,96},{64,0},{96,32},{1,65},{33,97},{65,1},{97,33},{2,66}... | collective-permute-start | bytes 466952 | tf_op jit(solution)/shard_map/ppermute | solution.py:449
  32.9 9.0 %collective-permute-start.7 = (bf16[528,128]{1,0:T(8,128)(2,1)}, bf16[528,128]{1,0:T(8,128)(2,1)S(1)}, u32[]{:S(2)}, u32[]{:S(2)}) collective-permute-start(bf16[528,128]{1,0:T(8,128)(2,1)} %get-tuple-element.42.refs_2_.refs_8_), channel_id=1, source_target_pairs={{0,1},{1,0},{2,3},{3,2},{4,5},{5,4},{6,7},{7,6},{8,9},{9,8},{10,11... | collective-permute-start | bytes 405512 | tf_op jit(solution)/shard_map/ppermute | solution.py:441
  35.9 6.1 %collective-permute-start.10 = (bf16[528,128]{1,0:T(8,128)(2,1)S(1)}, bf16[528,128]{1,0:T(8,128)(2,1)S(1)}, u32[]{:S(2)}, u32[]{:S(2)}) collective-permute-start(bf16[528,128]{1,0:T(8,128)(2,1)S(1)} %collective-permute-done.4.refs_5_), channel_id=1, source_target_pairs={{0,1},{1,0},{2,3},{3,2},{4,5},{5,4},{6,7},{7,6},{8,9},{9,8},{10,11... | collective-permute-start | bytes 405512 | tf_op jit(solution)/shard_map/ppermute | solution.py:441
  37.2 4.7 %collective-permute-start.9 = (bf16[528,128]{1,0:T(8,128)(2,1)S(1)}, bf16[528,128]{1,0:T(8,128)(2,1)S(1)}, u32[]{:S(2)}, u32[]{:S(2)}) collective-permute-start(bf16[528,128]{1,0:T(8,128)(2,1)S(1)} %collective-permute-done.3.refs_4_), channel_id=1, source_target_pairs={{0,1},{1,0},{2,3},{3,2},{4,5},{5,4},{6,7},{7,6},{8,9},{9,8},{10,11... | collective-permute-start | bytes 405512 | tf_op jit(solution)/shard_map/ppermute | solution.py:441
  37.2 4.7 %collective-permute-start.8 = (bf16[528,128]{1,0:T(8,128)(2,1)S(1)}, bf16[528,128]{1,0:T(8,128)(2,1)S(1)}, u32[]{:S(2)}, u32[]{:S(2)}) collective-permute-start(bf16[528,128]{1,0:T(8,128)(2,1)S(1)} %collective-permute-done.2.refs_3_), channel_id=1, source_target_pairs={{0,1},{1,0},{2,3},{3,2},{4,5},{5,4},{6,7},{7,6},{8,9},{9,8},{10,11... | collective-permute-start | bytes 405512 | tf_op jit(solution)/shard_map/ppermute | solution.py:441
  37.8 0.9 copy-start.2
  39.6 22.7 %copy-start.9 = (bf16[2,304,128]{2,1,0:T(8,128)(2,1)S(1)}, bf16[2,304,128]{2,1,0:T(8,128)(2,1)}, u32[]{:S(2)}) copy-start(bf16[2,304,128]{2,1,0:T(8,128)(2,1)} %stack_two.3.refs_2_) | copy-start | bytes 466948
  67.2 8.2 %collective-permute-start.12 = (bf16[4,512,128]{2,1,0:T(8,128)(2,1)S(1)}, bf16[4,512,128]{2,1,0:T(8,128)(2,1)S(1)}, u32[]{:S(2)}, u32[]{:S(2)}) collective-permute-start(bf16[4,512,128]{2,1,0:T(8,128)(2,1)S(1)} %get-tuple-element.60), channel_id=1, source_target_pairs={{0,1},{1,0},{2,3},{3,2},{4,5},{5,4},{6,7},{7,6},{8,9},{9,8},{10,11... | collective-permute-start | bytes 1572872 | tf_op jit(solution)/shard_map/ppermute | solution.py:441
  69.0 20.2 %copy-start = (bf16[4,128,4096]{2,1,0:T(8,128)(2,1)S(1)}, bf16[4,128,4096]{2,1,0:T(8,128)(2,1)}, u32[]{:S(2)}) copy-start(bf16[4,128,4096]{2,1,0:T(8,128)(2,1)} %param.9) | copy-start | bytes 12582916
  69.0 20.2 %copy-start.10 = (f32[768,128]{1,0:T(8,128)S(1)}, f32[768,128]{1,0:T(8,128)}, u32[]{:S(2)}) copy-start(f32[768,128]{1,0:T(8,128)} %get-tuple-element.54.raw_ref) | copy-start | bytes 1179652
  71.0 18.2 %copy-start.1 = (bf16[8,32,4096]{2,1,0:T(8,128)(2,1)S(1)}, bf16[8,32,4096]{2,1,0:T(8,128)(2,1)}, u32[]{:S(2)}) copy-start(bf16[8,32,4096]{2,1,0:T(8,128)(2,1)} %param.8) | copy-start | bytes 6291460
  71.0 18.2 %copy-start.12 = (s32[4]{0:T(128)S(1)}, s32[4]{0:T(128)}, u32[]{:S(2)}) copy-start(s32[4]{0:T(128)} %p_len_ref.3) | copy-start | bytes 52
  71.0 9.4 %collective-permute-start.15 = (bf16[2,256,128]{2,1,0:T(8,128)(2,1)S(1)}, bf16[2,256,128]{2,1,0:T(8,128)(2,1)S(1)}, u32[]{:S(2)}, u32[]{:S(2)}) collective-permute-start(bf16[2,256,128]{2,1,0:T(8,128)(2,1)S(1)} %get-tuple-element.67), channel_id=1, source_target_pairs={{0,16},{8,24},{16,0},{24,8},{1,17},{9,25},{17,1},{25,9},{2,18},{10... | collective-permute-start | bytes 393224 | tf_op jit(solution)/shard_map/ppermute | solution.py:449
  71.6 13.1 %collective-permute-start.13 = (bf16[2,256,128]{2,1,0:T(8,128)(2,1)S(1)}, bf16[2,256,128]{2,1,0:T(8,128)(2,1)S(1)}, u32[]{:S(2)}, u32[]{:S(2)}) collective-permute-start(bf16[2,256,128]{2,1,0:T(8,128)(2,1)S(1)} %get-tuple-element.63), channel_id=1, source_target_pairs={{0,64},{32,96},{64,0},{96,32},{1,65},{33,97},{65,1},{97,33},{2,66}... | collective-permute-start | bytes 393224 | tf_op jit(solution)/shard_map/ppermute | solution.py:449
  72.5 12.3 %collective-permute-start.20 = (bf16[512,128]{1,0:T(8,128)(2,1)S(1)}, bf16[512,128]{1,0:T(8,128)(2,1)S(1)}, u32[]{:S(2)}, u32[]{:S(2)}) collective-permute-start(bf16[512,128]{1,0:T(8,128)(2,1)S(1)} %get-tuple-element.73), channel_id=1, source_target_pairs={{0,128},{128,0},{1,129},{129,1},{2,130},{130,2},{3,131},{131,3},{4... | collective-permute-start | bytes 393224 | tf_op jit(solution)/shard_map/ppermute | solution.py:441
  75.6 13.6 %collective-permute-start.17 = (bf16[512,128]{1,0:T(8,128)(2,1)S(1)}, bf16[512,128]{1,0:T(8,128)(2,1)S(1)}, u32[]{:S(2)}, u32[]{:S(2)}) collective-permute-start(bf16[512,128]{1,0:T(8,128)(2,1)S(1)} %get-tuple-element.70), channel_id=1, source_target_pairs={{0,2},{2,0},{1,3},{3,1},{4,6},{6,4},{5,7},{7,5},{8,10},{10,8},{9,1... | collective-permute-start | bytes 393224 | tf_op jit(solution)/shard_map/ppermute | solution.py:441
  76.0 13.1 %collective-permute-start.18 = (bf16[512,128]{1,0:T(8,128)(2,1)S(1)}, bf16[512,128]{1,0:T(8,128)(2,1)S(1)}, u32[]{:S(2)}, u32[]{:S(2)}) collective-permute-start(bf16[512,128]{1,0:T(8,128)(2,1)S(1)} %get-tuple-element.71), channel_id=1, source_target_pairs={{0,4},{4,0},{1,5},{5,1},{2,6},{6,2},{3,7},{7,3},{8,12},{12,8},{9,1... | collective-permute-start | bytes 393224 | tf_op jit(solution)/shard_map/ppermute | solution.py:441
  80.4 8.8 %collective-permute-start.19 = (bf16[512,128]{1,0:T(8,128)(2,1)S(1)}, bf16[512,128]{1,0:T(8,128)(2,1)S(1)}, u32[]{:S(2)}, u32[]{:S(2)}) collective-permute-start(bf16[512,128]{1,0:T(8,128)(2,1)S(1)} %get-tuple-element.72), channel_id=1, source_target_pairs={{0,6},{2,4},{4,2},{6,0},{1,7},{3,5},{5,3},{7,1},{8,14},{10,12},{12... | collective-permute-start | bytes 393224 | tf_op jit(solution)/shard_map/ppermute | solution.py:445
  84.7 4.4 %collective-permute-start.16 = (bf16[256,128]{1,0:T(8,128)(2,1)S(1)}, bf16[256,128]{1,0:T(8,128)(2,1)S(1)}, u32[]{:S(2)}, u32[]{:S(2)}) collective-permute-start(bf16[256,128]{1,0:T(8,128)(2,1)S(1)} %get-tuple-element.69), channel_id=1, source_target_pairs={{0,8},{8,0},{16,24},{24,16},{1,9},{9,1},{17,25},{25,17},{2,10},{10... | collective-permute-start | bytes 196616 | tf_op jit(solution)/shard_map/ppermute | solution.py:449
  84.9 4.3 %collective-permute-start.14 = (bf16[256,128]{1,0:T(8,128)(2,1)S(1)}, bf16[256,128]{1,0:T(8,128)(2,1)S(1)}, u32[]{:S(2)}, u32[]{:S(2)}) collective-permute-start(bf16[256,128]{1,0:T(8,128)(2,1)S(1)} %get-tuple-element.65), channel_id=1, source_target_pairs={{0,32},{32,0},{64,96},{96,64},{1,33},{33,1},{65,97},{97,65},{2,34}... | collective-permute-start | bytes 196616 | tf_op jit(solution)/shard_map/ppermute | solution.py:449
  91.9 4.6 %collective-permute-start.21 = (bf16[32,80,128]{2,1,0:T(8,128)(2,1)S(1)}, bf16[32,80,128]{2,1,0:T(8,128)(2,1)S(1)}, u32[]{:S(2)}, u32[]{:S(2)}) collective-permute-start(bf16[32,80,128]{2,1,0:T(8,128)(2,1)S(1)} %get-tuple-element.75), channel_id=1, source_target_pairs={{0,1},{1,0},{2,3},{3,2},{4,5},{5,4},{6,7},{7,6},{8,9},{9,8},{10,11... | collective-permute-start | bytes 1966088 | tf_op jit(solution)/shard_map/ppermute | solution.py:441
  136.7 6.6 %collective-permute-start.22 = (bf16[32,64,128]{2,1,0:T(8,128)(2,1)S(1)}, bf16[32,64,128]{2,1,0:T(8,128)(2,1)S(1)}, u32[]{:S(2)}, u32[]{:S(2)}) collective-permute-start(bf16[32,64,128]{2,1,0:T(8,128)(2,1)S(1)} %all_to_all.23.x_ref), channel_id=1, source_target_pairs={{0,1},{1,0},{2,3},{3,2},{4,5},{5,4},{6,7},{7,6},{8,9},{9,8},{10,11... | collective-permute-start | bytes 1572872 | tf_op jit(solution)/shard_map/ppermute | solution.py:441
  (6 other events, 4.9 us)
